TPU v7x, 32 devices: a whole 2x2x4 slice. The times are simulated.
32 devices in a mesh: groups: 2 (over y), replica: 16 (over z, x, core).
Axes of the slice: x: 2, y: 2, z: 4, core: 2. Of those that a mesh axis runs over, the one named last changes fastest.
Arguments:
- hidden_state_rows: bfloat16 [3072, 8192], P(('groups', 'replica')), parts along dimension 0, may hold values from -6 to 6
- base_queries: bfloat16 [3072, 4096], P(('groups', 'replica')), parts along dimension 0, may hold values from -6 to 6
- cached_key_rows: bfloat16 [3072, 32, 512], P(('groups', 'replica')), parts along dimension 0, may hold values from -600 to 600
- cached_value_rows: bfloat16 [3072, 32, 512], P(('groups', 'replica')), parts along dimension 0, may hold values from -6 to 6
- cache_lengths: int32 [3072], P(('groups', 'replica')), parts along dimension 0, may hold values from 16 to 32, as said below
- joining_flags: int32 [3072], P(('groups', 'replica')), parts along dimension 0, may hold values 0 or 1
- adapter_index: int32 [3072, 1], P(('groups', 'replica')), parts along dimension 0, may hold values from 0 to 15; in each aligned block of 96 rows (0 to 95, 96 to 191, ...) at most 12 rows name the same one
- adapter_owner_row: int32 [16], replicated, may hold values from 0 to 15, each once
- pair_trade_flags: int32 [16], P('groups'), parts along dimension 0, may hold values 0 or 1
- down_factors: bfloat16 [16, 8192, 64], P('replica'), may hold values from -0.0625 to 0.0625
- up_factors: bfloat16 [16, 64, 4096], P('replica'), may hold values from -0.75 to 0.75
Outputs:
- attn_out: bfloat16 [3072, 4096], P(('groups', 'replica')), parts along dimension 0
There are 2 independent parts, one for each index of `groups`. A program takes and returns all parts, laid end to end along the dimension named above; an argument that names none is the same for every part. Nothing has to cross between parts.
Inputs may be any that keep to these rules, and one draw needn't show every extreme that they name: `adapter_index`: within the requests of one replica (aligned blocks of 96 rows) no adapter is named more than 12 times, a bound that some block reaches. `adapter_owner_row`: A permutation of the adapters. `cache_lengths`: the first request of each replica has 32 live positions, the second 16.
All inputs are finite; a program needn't handle non-finite values. No bound on the sum of `joining_flags` on one device may be relied on, other than what follows from the above.
Results may differ from a plain program's by a relative error of at most 0.0052.
Values may be sent and summed in bfloat16 or wider, within the bound.
A program may use at most 64 MiB of HBM per device.

v0:
```python
import math

import jax
import jax.numpy as jnp
from jax import lax
from jax.sharding import PartitionSpec as P

QUERY_HEADS = 32
KEY_HEADS = 4
HEAD_WIDTH = 128
SPAN = 16


ADAPTER_SCALE = 0.5
NEG_LARGE = -1e30


def swapped(block, axis, bit):
    count = lax.axis_size(axis)
    route = []
    for low in range(count):
        high = low | 1 << bit
        if high != low and high < count:
            route += [(low, high), (high, low)]
    return lax.ppermute(block, axis, route)


def attend(
    base_queries, query_shift, cached_key_rows, cached_value_rows, cache_lengths, joining_flags
):
    total_rows = base_queries.shape[0]
    cache_positions = cached_key_rows.shape[1]
    heads_per_group = QUERY_HEADS // KEY_HEADS
    base_share = base_queries.reshape(total_rows, KEY_HEADS, heads_per_group, HEAD_WIDTH)
    adapter_share = query_shift.reshape(total_rows, KEY_HEADS, heads_per_group, HEAD_WIDTH)
    keys_from_cache = cached_key_rows.reshape(total_rows, cache_positions, KEY_HEADS, HEAD_WIDTH)
    values_from_cache = cached_value_rows.reshape(
        total_rows, cache_positions, KEY_HEADS, HEAD_WIDTH
    )
    scores = jnp.einsum(
        "rkgd,rpkd->rkgp", base_share, keys_from_cache, preferred_element_type=jnp.float32
    )
    scores = scores + jnp.einsum(
        "rkgd,rpkd->rkgp", adapter_share, keys_from_cache, preferred_element_type=jnp.float32
    )
    scores = scores / math.sqrt(HEAD_WIDTH)
    position = jnp.arange(cache_positions, dtype=jnp.int32)[None, :]
    limits = cache_lengths[:, None]
    visible = (position < limits) & ((joining_flags[:, None] == 0) | (position >= limits - SPAN))
    visible = visible[:, None, None, :]
    masked = jnp.where(visible, scores, NEG_LARGE)
    row_top = jnp.max(masked, axis=-1, keepdims=True)
    raised = jnp.where(visible, jnp.exp(masked - row_top), 0.0)
    weights = (raised / jnp.sum(raised, axis=-1, keepdims=True)).astype(jnp.bfloat16)
    mixed_out = jnp.einsum(
        "rkgp,rpkd->rkgd", weights, values_from_cache, preferred_element_type=jnp.float32
    )
    return mixed_out.astype(jnp.bfloat16).reshape(total_rows, QUERY_HEADS * HEAD_WIDTH)


def routed_rows(hidden_state_rows, adapter_index, adapter_owner_row, down_factors, up_factors):
    replicas = lax.axis_size("replica")
    total_rows = hidden_state_rows.shape[0]
    capacity = max(2, (2 * total_rows + replicas - 1) // replicas)
    adapter_column = adapter_index[:, 0]
    table = jnp.arange(adapter_owner_row.shape[0], dtype=jnp.int32)
    stores = jnp.sum(
        jnp.where(adapter_column[:, None] == table[None, :], adapter_owner_row[None, :], 0), axis=1
    )
    order = jnp.arange(total_rows, dtype=jnp.int32)
    earlier = (stores[:, None] == stores[None, :]) & (order[None, :] < order[:, None])
    slot_index = jnp.sum(earlier.astype(jnp.int32), axis=1)
    target = stores * capacity + slot_index
    slots = jnp.arange(replicas * capacity, dtype=jnp.int32)
    placing = (slots[:, None] == target[None, :]).astype(jnp.bfloat16)
    outgoing = jnp.dot(placing, hidden_state_rows, preferred_element_type=jnp.float32).astype(
        jnp.bfloat16
    )
    outgoing = outgoing.reshape(replicas, capacity, hidden_state_rows.shape[1])
    down_factor_here = down_factors[0]
    up_factor_here = up_factors[0]
    arrived = lax.all_to_all(outgoing, "replica", split_axis=0, concat_axis=0, tiled=True)
    sources = arrived.shape[0]
    items = arrived.shape[1]
    flat_rows = arrived.reshape(sources * items, arrived.shape[2])
    narrowed_rows = jnp.dot(flat_rows, down_factor_here, preferred_element_type=jnp.float32).astype(
        jnp.bfloat16
    )
    widened_rows = (
        ADAPTER_SCALE * jnp.dot(narrowed_rows, up_factor_here, preferred_element_type=jnp.float32)
    ).astype(jnp.bfloat16)
    computed = widened_rows.reshape(sources, items, widened_rows.shape[1])
    returned = lax.all_to_all(computed, "replica", split_axis=0, concat_axis=0, tiled=True)
    returned = returned.reshape(replicas * capacity, returned.shape[2])
    picked = jnp.einsum("sr,sq->rq", placing, returned, preferred_element_type=jnp.float32)
    return picked.astype(jnp.bfloat16)


def per_device(
    hidden_state_rows,
    base_queries,
    cached_key_rows,
    cached_value_rows,
    cache_lengths,
    joining_flags,
    adapter_index,
    adapter_owner_row,
    pair_trade_flags,
    down_factors,
    up_factors,
):
    here = lax.axis_index("replica")
    trade = lax.dynamic_index_in_dim(pair_trade_flags, here // 2, 0, keepdims=False) == 1
    arrived = swapped(
        (hidden_state_rows, base_queries, cached_key_rows, cached_value_rows), "replica", 0
    )
    request_details = jnp.stack([cache_lengths, joining_flags, adapter_index[:, 0]], axis=1)
    arrived_details = swapped(request_details, "replica", 0)
    hidden_state_rows = jnp.where(trade, arrived[0], hidden_state_rows)
    base_queries = jnp.where(trade, arrived[1], base_queries)
    cached_key_rows = jnp.where(trade, arrived[2], cached_key_rows)
    cached_value_rows = jnp.where(trade, arrived[3], cached_value_rows)
    request_details = jnp.where(trade, arrived_details, request_details)
    query_shift = routed_rows(
        hidden_state_rows, request_details[:, 2:3], adapter_owner_row, down_factors, up_factors
    )
    return attend(
        base_queries,
        query_shift,
        cached_key_rows,
        cached_value_rows,
        request_details[:, 0],
        request_details[:, 1],
    )


def solution(mesh):
    placed = (
        P(("groups", "replica"), None),
        P(("groups", "replica"), None),
        P(("groups", "replica"), None, None),
        P(("groups", "replica"), None, None),
        P(("groups", "replica")),
        P(("groups", "replica")),
        P(("groups", "replica"), None),
        P(),
        P("groups"),
        P("replica", None, None),
        P("replica", None, None),
    )
    return jax.shard_map(
        per_device,
        mesh=mesh,
        in_specs=placed,
        out_specs=P(("groups", "replica"), None),
        check_vma=False,
    )
```

profile of v0, /device:TPU:20, one launch (start us, length us, event | category | flops | bytes accessed | tf_op | source)
XLA Modules:
  0.0 193.2 jit_solution(8265742040448307838)
XLA Ops:
  0.0 0.0 copy-start
  0.0 0.0 collective-permute-start.3
  0.0 0.8 pad_add_fusion
  0.8 0.5 collective-permute-start
  1.3 1.2 dynamic_slice.4
  3.2 0.3 collective-permute-done
  3.4 0.7 broadcast_select_fusion
  4.1 0.7 select_reduce_fusion
  4.9 0.2 convert_reduce_fusion
  5.0 0.0 collective-permute-done.3
  5.1 2.6 %convolution_convert_fusion = bf16[192,8192]{1,0:T(8,128)(2,1)} fusion(bf16[96,8192]{1,0:T(8,128)(2,1)S(1)} %collective-permute-done.3, bf16[96,8192]{1,0:T(8,128)(2,1)} %param.11, pred[]{:T(512)} %bitcast, s32[96]{0:T(128)S(1)} %multiply_add_fusion), kind=kOutput, calls=%fused_computation.1 | convolution fusion | flops 304367616 | bytes 6291841 | tf_op jit(solution)/shard_map/dot_general | solution.py:76
  7.7 4.7 %reshape.92 = bf16[16,12,8192]{2,1,0:T(8,128)(2,1)} reshape(bf16[192,8192]{1,0:T(8,128)(2,1)} %convolution_convert_fusion) | data formatting | bytes 6291456 | tf_op jit(solution)/shard_map/reshape | solution.py:79
  12.4 7.6 %all-to-all-start = ((bf16[16,12,8192]{2,1,0:T(8,128)(2,1)}), bf16[16,12,8192]{2,1,0:T(8,128)(2,1)}, u32[]{:S(2)}, u32[]{:S(2)}) async-start(bf16[16,12,8192]{2,1,0:T(8,128)(2,1)} %reshape.92), calls=%async_computation | async-start | bytes 8388608 | tf_op jit(solution)/shard_map/all_to_all | solution.py:82
  19.9 0.0 copy-start.3
  19.9 0.2 collective-permute-start.2
  20.2 92.5 %all-to-all-done = bf16[16,12,8192]{2,1,0:T(8,128)(2,1)} async-done(((bf16[16,12,8192]{2,1,0:T(8,128)(2,1)}), bf16[16,12,8192]{2,1,0:T(8,128)(2,1)}, u32[]{:S(2)}, u32[]{:S(2)}) %all-to-all-start) | async-done | bytes 3145760 | tf_op jit(solution)/shard_map/all_to_all | solution.py:82
  112.6 4.7 %reshape.93 = bf16[192,8192]{1,0:T(8,128)(2,1)} reshape(bf16[16,12,8192]{2,1,0:T(8,128)(2,1)} %all-to-all-done) | data formatting | bytes 6291456 | tf_op jit(solution)/shard_map/reshape | solution.py:85
  117.4 0.0 copy-done
  117.4 0.0 copy-done.3
  117.4 4.3 %fusion.1 = bf16[192,4096]{1,0:T(8,128)(2,1)S(1)} fusion(bf16[192,8192]{1,0:T(8,128)(2,1)} %reshape.93, bf16[1,8192,64]{1,2,0:T(8,128)(2,1)S(1)} %copy-done, bf16[1,64,4096]{2,1,0:T(8,128)(2,1)S(1)} %copy-done.3), kind=kOutput, calls=%fused_computation.3 | convolution fusion | flops 303575040 | bytes 6291456 | tf_op jit(solution)/shard_map/dot_general | solution.py:90
  121.7 1.6 reshape.94
  123.2 4.7 %all-to-all-start.1 = ((bf16[16,12,4096]{2,1,0:T(8,128)(2,1)}), bf16[16,12,4096]{2,1,0:T(8,128)(2,1)S(1)}, u32[]{:S(2)}, u32[]{:S(2)}) async-start(bf16[16,12,4096]{2,1,0:T(8,128)(2,1)} %reshape.94), calls=%async_computation.1 | async-start | bytes 4194304 | tf_op jit(solution)/shard_map/all_to_all | solution.py:93
  127.9 0.1 collective-permute-start.4
  128.1 0.4 collective-permute-start.1
  128.4 0.1 fusion.26
  128.5 6.2 %collective-permute-done.1 = bf16[96,4096]{1,0:T(8,128)(2,1)S(1)} collective-permute-done((bf16[96,4096]{1,0:T(8,128)(2,1)}, bf16[96,4096]{1,0:T(8,128)(2,1)S(1)}, u32[]{:S(2)}, u32[]{:S(2)}) %collective-permute-start.1) | collective-permute-done | bytes 786464 | tf_op jit(solution)/shard_map/ppermute | solution.py:25
  134.7 0.1 select_bitcast_fusion.2
  134.8 1.0 copy.23
  135.8 39.7 %all-to-all-done.1 = bf16[16,12,4096]{2,1,0:T(8,128)(2,1)S(1)} async-done(((bf16[16,12,4096]{2,1,0:T(8,128)(2,1)}), bf16[16,12,4096]{2,1,0:T(8,128)(2,1)S(1)}, u32[]{:S(2)}, u32[]{:S(2)}) %all-to-all-start.1) | async-done | bytes 1572896 | tf_op jit(solution)/shard_map/all_to_all | solution.py:93
  175.6 1.3 reshape.95
  176.9 0.0 copy-start.1
  176.9 2.0 %fusion.19 = bf16[12,8,32,128]{3,1,2,0:T(8,128)(2,1)S(1)} fusion(bf16[192,4096]{1,0:T(8,128)(2,1)} %reshape.95, s32[96]{0:T(128)S(1)} %multiply_add_fusion), kind=kOutput, calls=%fused_computation.23 | convolution fusion | flops 151406592 | bytes 2359680 | tf_op jit(solution)/shard_map/sr,sq->rq/dot_general | solution.py:95
  178.9 0.2 copy.24
  179.0 0.0 collective-permute-done.2
  179.0 0.2 copy-done.1
  179.2 0.0 copy-start.2
  179.2 3.7 %fusion.5 = f32[96,4,8,32]{3,2,1,0:T(8,128)S(1)} fusion(bf16[96,4,8,128]{3,2,1,0:T(8,128)(2,1)S(1)} %bitcast.60, bf16[96,32,512]{2,1,0:T(8,128)(2,1)} %collective-permute-done.2, bf16[96,32,512]{2,1,0:T(8,128)(2,1)S(1)} %copy-done.1, pred[]{:T(512)} %bitcast), kind=kOutput, calls=%fused_computation.8 | convolution fusion | flops 26738688 | bytes 7471105 | tf_op jit(solution)/shard_map/rkgd,rpkd->rkgp/dot_general | solution.py:43
  182.9 0.0 copy-done.2
  182.9 5.6 %fusion.29 = (f32[96,4,8]{2,1,0:T(4,128)}, f32[96,4,8,32]{3,2,1,0:T(8,128)}) fusion(pred[96,32]{1,0:T(8,128)(4,1)S(1)} %fusion.26, f32[96,4,8,32]{3,2,1,0:T(8,128)S(1)} %fusion.5, bf16[96,4,8,128]{3,2,1,0:T(8,128)(2,1)S(1)} %bitcast.61, bf16[96,32,512]{2,1,0:T(8,128)(2,1)} %collective-permute-done.2, bf16[96,32,512]{2,1,0:T(8,128)(2,1)} %param.13, pred[]{:T(512)} %bitcast), kind=kOutput, calls=%fused_computation.49 | convolution fusion | flops 27328544 | bytes 7879681 | tf_op jit(solution)/shard_map/sub | solution.py:53
  188.6 0.0 collective-permute-done.4
  188.6 3.5 %fusion.16 = bf16[96,4,8,128]{3,2,1,0:T(8,128)(2,1)S(1)} fusion(f32[96,4,8,32]{3,2,1,0:T(8,128)} %get-tuple-element.9, f32[96,4,8]{2,1,0:T(4,128)} %get-tuple-element.8, bf16[96,32,512]{2,1,0:T(8,128)(2,1)} %collective-permute-done.4, bf16[96,32,512]{2,1,0:T(8,128)(2,1)} %param.14, pred[]{:T(512)} %bitcast), kind=kOutput, calls=%fused_computation.22 | convolution fusion | flops 27328512 | bytes 7483393 | tf_op jit(solution)/shard_map/rkgp,rpkd->rkgd/dot_general | solution.py:55
  192.0 1.2 copy.45
  (3 shorter events, 0.0 us)
Async XLA Ops:
  0.0 117.4 %copy-start = (bf16[1,8192,64]{1,2,0:T(8,128)(2,1)S(1)}, bf16[1,8192,64]{1,2,0:T(8,128)(2,1)}, u32[]{:S(2)}) copy-start(bf16[1,8192,64]{1,2,0:T(8,128)(2,1)} %param.20) | copy-start | bytes 3145732
  0.0 5.0 %collective-permute-start.3 = (bf16[96,8192]{1,0:T(8,128)(2,1)}, bf16[96,8192]{1,0:T(8,128)(2,1)S(1)}, u32[]{:S(2)}, u32[]{:S(2)}) collective-permute-start(bf16[96,8192]{1,0:T(8,128)(2,1)} %param.11), channel_id=1, source_target_pairs={{0,1},{1,0},{2,3},{3,2},{4,5},{5,4},{6,7},{7,6},{8,9},{9,8},{10,11... | collective-permute-start | bytes 4718600 | tf_op jit(solution)/shard_map/ppermute | solution.py:25
  0.8 2.6 %collective-permute-start = (s32[96,3]{0,1:T(4,128)S(1)}, s32[96,3]{0,1:T(4,128)S(1)}, u32[]{:S(2)}, u32[]{:S(2)}) collective-permute-start(s32[96,3]{0,1:T(4,128)S(1)} %pad_add_fusion), channel_id=1, source_target_pairs={{0,1},{1,0},{2,3},{3,2},{4,5},{5,4},{6,7},{7,6},{8,9},{9,8},{10,11... | collective-permute-start | bytes 3464 | tf_op jit(solution)/shard_map/ppermute | solution.py:25
  12.4 100.3 %all-to-all-start = ((bf16[16,12,8192]{2,1,0:T(8,128)(2,1)}), bf16[16,12,8192]{2,1,0:T(8,128)(2,1)}, u32[]{:S(2)}, u32[]{:S(2)}) async-start(bf16[16,12,8192]{2,1,0:T(8,128)(2,1)} %reshape.92), calls=%async_computation | async-start | bytes 8388608 | tf_op jit(solution)/shard_map/all_to_all | solution.py:82
  19.9 97.4 %copy-start.3 = (bf16[1,64,4096]{2,1,0:T(8,128)(2,1)S(1)}, bf16[1,64,4096]{2,1,0:T(8,128)(2,1)}, u32[]{:S(2)}) copy-start(bf16[1,64,4096]{2,1,0:T(8,128)(2,1)} %param.21) | copy-start | bytes 1572868
  19.9 159.1 %collective-permute-start.2 = (bf16[96,32,512]{2,1,0:T(8,128)(2,1)}, bf16[96,32,512]{2,1,0:T(8,128)(2,1)}, u32[]{:S(2)}, u32[]{:S(2)}) collective-permute-start(bf16[96,32,512]{2,1,0:T(8,128)(2,1)} %param.13), channel_id=1, source_target_pairs={{0,1},{1,0},{2,3},{3,2},{4,5},{5,4},{6,7},{7,6},{8,9},{9,8},{10,11... | collective-permute-start | bytes 9437192 | tf_op jit(solution)/shard_map/ppermute | solution.py:25
  123.2 52.3 %all-to-all-start.1 = ((bf16[16,12,4096]{2,1,0:T(8,128)(2,1)}), bf16[16,12,4096]{2,1,0:T(8,128)(2,1)S(1)}, u32[]{:S(2)}, u32[]{:S(2)}) async-start(bf16[16,12,4096]{2,1,0:T(8,128)(2,1)} %reshape.94), calls=%async_computation.1 | async-start | bytes 4194304 | tf_op jit(solution)/shard_map/all_to_all | solution.py:93
  127.9 60.7 %collective-permute-start.4 = (bf16[96,32,512]{2,1,0:T(8,128)(2,1)}, bf16[96,32,512]{2,1,0:T(8,128)(2,1)}, u32[]{:S(2)}, u32[]{:S(2)}) collective-permute-start(bf16[96,32,512]{2,1,0:T(8,128)(2,1)} %param.14), channel_id=1, source_target_pairs={{0,1},{1,0},{2,3},{3,2},{4,5},{5,4},{6,7},{7,6},{8,9},{9,8},{10,11... | collective-permute-start | bytes 9437192 | tf_op jit(solution)/shard_map/ppermute | solution.py:25
  128.1 6.7 %collective-permute-start.1 = (bf16[96,4096]{1,0:T(8,128)(2,1)}, bf16[96,4096]{1,0:T(8,128)(2,1)S(1)}, u32[]{:S(2)}, u32[]{:S(2)}) collective-permute-start(bf16[96,4096]{1,0:T(8,128)(2,1)} %param.12), channel_id=1, source_target_pairs={{0,1},{1,0},{2,3},{3,2},{4,5},{5,4},{6,7},{7,6},{8,9},{9,8},{10,11... | collective-permute-start | bytes 2359304 | tf_op jit(solution)/shard_map/ppermute | solution.py:25
  176.9 2.4 %copy-start.1 = (bf16[96,32,512]{2,1,0:T(8,128)(2,1)S(1)}, bf16[96,32,512]{2,1,0:T(8,128)(2,1)}, u32[]{:S(2)}) copy-start(bf16[96,32,512]{2,1,0:T(8,128)(2,1)} %param.13) | copy-start | bytes 9437188
  179.2 3.7 %copy-start.2 = (bf16[12,8,32,128]{3,2,1,0:T(8,128)(2,1)S(1)}, bf16[12,8,32,128]{3,2,1,0:T(8,128)(2,1)}, u32[]{:S(2)}) copy-start(bf16[12,8,32,128]{3,2,1,0:T(8,128)(2,1)} %copy.23) | copy-start | bytes 2359300
where the time goes:
time: 193 us
  waiting for transfers between devices  139 us (72%)
  matrix products  21.7 us (11%)
  local copies, waits for them, and re-layouts  16.1 us (8%)
  starting transfers between devices  13.4 us (7%)
  other arithmetic  2.61 us (1%)
    all_to_all x1, waiting for transfers between devices, routed_rows(): lax.all_to_all(outgoing, 'replica', split_axis=0, concat_axis=0, tiled=True)  92.5 us
    all_to_all x1, waiting for transfers between devices, routed_rows(): lax.all_to_all(computed, 'replica', split_axis=0, concat_axis=0, tiled=True)  39.7 us
    all_to_all x1, starting transfers between devices, routed_rows(): lax.all_to_all(outgoing, 'replica', split_axis=0, concat_axis=0, tiled=True)  7.56 us
    ppermute x5, waiting for transfers between devices, swapped(): return lax.ppermute(block, axis, route)  6.44 us
    sub x1, matrix products, attend(): raised = jnp.where(visible, jnp.exp(masked - row_top), 0.0)  5.62 us
    reshape x1, local copies, waits for them, and re-layouts, routed_rows(): flat_rows = arrived.reshape(sources * items, arrived.shape[2])  4.72 us
    reshape x1, local copies, waits for them, and re-layouts, routed_rows(): outgoing = outgoing.reshape(replicas, capacity, hidden_state_rows.shape[1])  4.69 us
    all_to_all x1, starting transfers between devices, routed_rows(): lax.all_to_all(computed, 'replica', split_axis=0, concat_axis=0, tiled=True)  4.68 us
  transfers between devices with their start and end apart: 7, of which 4 were waited for; matrix products, arithmetic and copies ran while one was open for 15% of the time, Pallas kernels for 0%

commit v1 on v0

v1 whole, which is shorter than its diff:
```python
import functools
import math

import jax
import jax.numpy as jnp
from jax import lax
from jax.experimental import pallas as pl
from jax.experimental.pallas import tpu as pltpu
from jax.sharding import PartitionSpec as P

QUERY_HEADS = 32
KEY_HEADS = 4
HEAD_WIDTH = 128
SPAN = 16
ADAPTER_SCALE = 0.5
NEG_LARGE = -1e30

STEP_ROWS = 16
HALF_ROWS = 8


def attend_kernel(lengths_ref, joins_ref, q_ref, d_ref, k_ref, v_ref, o_ref):
    positions = k_ref.shape[0] // STEP_ROWS
    per_group = QUERY_HEADS // KEY_HEADS
    keys = HALF_ROWS * positions
    rows = per_group * HALF_ROWS
    scale = 1.0 / math.sqrt(HEAD_WIDTH)
    row_request = lax.broadcasted_iota(jnp.int32, (rows, keys), 0) % HALF_ROWS
    column = lax.broadcasted_iota(jnp.int32, (rows, keys), 1)
    own = row_request == column // positions
    position = column % positions
    halves = []
    for half in range(2):
        limits = lengths_ref[0, half * HALF_ROWS : (half + 1) * HALF_ROWS, 0:1]
        joins = joins_ref[0, half * HALF_ROWS : (half + 1) * HALF_ROWS, 0:1]
        low = jnp.where(joins == 0, 0, limits - SPAN)
        limits = jnp.concatenate([limits] * per_group, axis=0)
        low = jnp.concatenate([low] * per_group, axis=0)
        visible = own & (position < limits) & (position >= low)
        outs = []
        for group in range(KEY_HEADS):
            lanes = pl.ds(group * HEAD_WIDTH, HEAD_WIDTH)
            key_block = k_ref[pl.ds(half * keys, keys), lanes]
            value_block = v_ref[pl.ds(half * keys, keys), lanes]
            pieces = []
            for ref in (q_ref, d_ref):
                for head in range(per_group):
                    at = (group * per_group + head) * HEAD_WIDTH
                    piece = ref[:, pl.ds(at, HEAD_WIDTH)].astype(jnp.float32)
                    pieces.append(piece[half * HALF_ROWS : (half + 1) * HALF_ROWS])
            queries = jnp.concatenate(pieces, axis=0).astype(jnp.bfloat16)
            both = lax.dot_general(
                queries, key_block, (((1,), (1,)), ((), ())), preferred_element_type=jnp.float32
            )
            scores = (both[:rows] + both[rows:]) * scale
            scores = jnp.where(visible, scores, NEG_LARGE)
            top = jnp.max(scores, axis=1, keepdims=True)
            raised = jnp.where(visible, jnp.exp(scores - top), 0.0)
            total = jnp.sum(raised, axis=1, keepdims=True)
            weights = (raised / total).astype(jnp.bfloat16)
            outs.append(jnp.dot(weights, value_block, preferred_element_type=jnp.float32))
        halves.append(outs)
    for group in range(KEY_HEADS):
        for head in range(per_group):
            at = (group * per_group + head) * HEAD_WIDTH
            span = slice(head * HALF_ROWS, (head + 1) * HALF_ROWS)
            tile = jnp.concatenate([halves[0][group][span], halves[1][group][span]], axis=0)
            o_ref[:, pl.ds(at, HEAD_WIDTH)] = tile.astype(o_ref.dtype)


def attend(base_queries, query_shift, keys, values, cache_lengths, joining_flags):
    rows, width = base_queries.shape
    positions, cache_width = keys.shape[1:]
    steps = rows // STEP_ROWS
    keys = keys.reshape(rows * positions, cache_width)
    values = values.reshape(rows * positions, cache_width)
    lengths = jnp.broadcast_to(cache_lengths.reshape(steps, STEP_ROWS, 1), (steps, STEP_ROWS, 128))
    joins = jnp.broadcast_to(joining_flags.reshape(steps, STEP_ROWS, 1), (steps, STEP_ROWS, 128))
    small = pl.BlockSpec((1, STEP_ROWS, 128), lambda i: (i, 0, 0))
    wide = pl.BlockSpec((STEP_ROWS, width), lambda i: (i, 0))
    cache = pl.BlockSpec((STEP_ROWS * positions, cache_width), lambda i: (i, 0))
    return pl.pallas_call(
        attend_kernel,
        grid=(steps,),
        in_specs=[small, small, wide, wide, cache, cache],
        out_specs=wide,
        out_shape=jax.ShapeDtypeStruct((rows, width), jnp.bfloat16),
        compiler_params=pltpu.CompilerParams(vmem_limit_bytes=32 * 1024 * 1024),
        cost_estimate=pl.CostEstimate(
            flops=2 * 3 * rows * positions * HALF_ROWS * width,
            bytes_accessed=2 * (keys.size + values.size + 3 * rows * width),
            transcendentals=rows * positions * QUERY_HEADS * HALF_ROWS,
        ),
    )(lengths, joins, base_queries, query_shift, keys, values)


def swapped(block, axis, bit):
    count = lax.axis_size(axis)
    route = []
    for low in range(count):
        high = low | 1 << bit
        if high != low and high < count:
            route += [(low, high), (high, low)]
    return lax.ppermute(block, axis, route)


def stores_of(adapter_index, adapter_owner_row):
    adapter_column = adapter_index[:, 0]
    table = jnp.arange(adapter_owner_row.shape[0], dtype=jnp.int32)
    return jnp.sum(
        jnp.where(adapter_column[:, None] == table[None, :], adapter_owner_row[None, :], 0), axis=1
    )


def routed_rows(hidden_state_rows, stores, down_factors, up_factors):
    replicas = lax.axis_size("replica")
    total_rows = hidden_state_rows.shape[0]
    capacity = max(2, (2 * total_rows + replicas - 1) // replicas)
    order = jnp.arange(total_rows, dtype=jnp.int32)
    earlier = (stores[:, None] == stores[None, :]) & (order[None, :] < order[:, None])
    slot_index = jnp.sum(earlier.astype(jnp.int32), axis=1)
    target = stores * capacity + slot_index
    slots = jnp.arange(replicas * capacity, dtype=jnp.int32)
    placing = (slots[:, None] == target[None, :]).astype(jnp.bfloat16)
    outgoing = jnp.dot(placing, hidden_state_rows, preferred_element_type=jnp.float32).astype(
        jnp.bfloat16
    )
    outgoing = outgoing.reshape(replicas, capacity, hidden_state_rows.shape[1])
    arrived = lax.all_to_all(outgoing, "replica", split_axis=0, concat_axis=0, tiled=True)
    sources = arrived.shape[0]
    items = arrived.shape[1]
    flat_rows = arrived.reshape(sources * items, arrived.shape[2])
    narrowed_rows = jnp.dot(flat_rows, down_factors[0], preferred_element_type=jnp.float32).astype(
        jnp.bfloat16
    )
    widened_rows = (
        ADAPTER_SCALE * jnp.dot(narrowed_rows, up_factors[0], preferred_element_type=jnp.float32)
    ).astype(jnp.bfloat16)
    computed = widened_rows.reshape(sources, items, widened_rows.shape[1])
    returned = lax.all_to_all(computed, "replica", split_axis=0, concat_axis=0, tiled=True)
    returned = returned.reshape(replicas * capacity, returned.shape[2])
    picked = jnp.einsum("sr,sq->rq", placing, returned, preferred_element_type=jnp.float32)
    return picked.astype(jnp.bfloat16)


def per_device(
    hidden_state_rows,
    base_queries,
    cached_key_rows,
    cached_value_rows,
    cache_lengths,
    joining_flags,
    adapter_index,
    adapter_owner_row,
    pair_trade_flags,
    down_factors,
    up_factors,
):
    here = lax.axis_index("replica")
    trade = lax.dynamic_index_in_dim(pair_trade_flags, here // 2, 0, keepdims=False) == 1
    stores = stores_of(adapter_index, adapter_owner_row)
    query_shift = routed_rows(hidden_state_rows, stores, down_factors, up_factors)
    attended = attend(
        base_queries,
        query_shift,
        cached_key_rows,
        cached_value_rows,
        cache_lengths,
        joining_flags,
    )
    return jnp.where(trade, swapped(attended, "replica", 0), attended)


def solution(mesh):
    placed = (
        P(("groups", "replica"), None),
        P(("groups", "replica"), None),
        P(("groups", "replica"), None, None),
        P(("groups", "replica"), None, None),
        P(("groups", "replica")),
        P(("groups", "replica")),
        P(("groups", "replica"), None),
        P(),
        P("groups"),
        P("replica", None, None),
        P("replica", None, None),
    )
    return jax.shard_map(
        per_device,
        mesh=mesh,
        in_specs=placed,
        out_specs=P(("groups", "replica"), None),
        check_vma=False,
    )
```

time: 193 us -> 197 us (1.021)
  the two profiles are of different devices: /device:TPU:20 before, /device:TPU:17 now
where the time goes in v1:
time: 197 us; the launch traced here: 196 us
  blocking collectives  98.5 us (50%)
  waiting for transfers between devices  47.7 us (24%)
  local copies, waits for them, and re-layouts  19.5 us (10%)
  Pallas kernels  12 us (6%)
  matrix products  9.2 us (5%)
  starting transfers between devices  6.62 us (3%)
  other arithmetic  2.02 us (1%)
    all_to_all x1, blocking collectives, routed_rows(): lax.all_to_all(outgoing, 'replica', split_axis=0, concat_axis=0, tiled=True)  98.5 us
    all_to_all x1, waiting for transfers between devices, routed_rows(): lax.all_to_all(computed, 'replica', split_axis=0, concat_axis=0, tiled=True)  47.1 us
    pallas_call x1, Pallas kernels, attend(): pl.pallas_call(attend_kernel, grid=(steps,), in_specs=[small, small, wide...  12 us
    all_to_all x1, starting transfers between devices, routed_rows(): lax.all_to_all(computed, 'replica', split_axis=0, concat_axis=0, tiled=True)  5.68 us
    dot_general x1, matrix products, routed_rows(): jnp.dot(narrowed_rows, up_factors[0], preferred_element_type=jnp.float32)  4.73 us
    reshape x1, local copies, waits for them, and re-layouts, routed_rows(): flat_rows = arrived.reshape(sources * items, arrived.shape[2])  4.69 us
    reshape x1, local copies, waits for them, and re-layouts, routed_rows(): outgoing = outgoing.reshape(replicas, capacity, hidden_state_rows.shape[1])  4.67 us
    unnamed x14, local copies, waits for them, and re-layouts  4.18 us
  transfers between devices with their start and end apart: 2, of which 2 were waited for; matrix products, arithmetic and copies ran while one was open for 0% of the time, Pallas kernels for 0%

profile of v1, /device:TPU:17, one launch (start us, length us, event | category | flops | bytes accessed | tf_op | source)
XLA Modules:
  0.0 196.3 jit_solution(64266306732548303)
XLA Ops:
  0.0 0.0 copy-start
  0.0 0.9 select_reduce_fusion
  0.9 0.2 convert_reduce_fusion
  1.1 0.4 copy-done
  1.4 2.6 %convolution_convert_fusion = bf16[192,8192]{1,0:T(8,128)(2,1)} fusion(bf16[96,8192]{1,0:T(8,128)(2,1)S(1)} %copy-done, s32[96]{0:T(128)S(1)} %multiply_add_fusion), kind=kOutput, calls=%fused_computation | convolution fusion | flops 303581184 | bytes 4718976 | tf_op jit(solution)/shard_map/dot_general | solution.py:125
  4.1 4.7 %reshape.33 = bf16[16,12,8192]{2,1,0:T(8,128)(2,1)} reshape(bf16[192,8192]{1,0:T(8,128)(2,1)} %convolution_convert_fusion) | data formatting | bytes 6291456 | tf_op jit(solution)/shard_map/reshape | solution.py:128
  8.8 98.5 %all_to_all.10 = bf16[16,12,8192]{2,1,0:T(8,128)(2,1)} all-to-all(bf16[16,12,8192]{2,1,0:T(8,128)(2,1)} %reshape.33), channel_id=1, replica_groups=mesh['groups'=2,'replica'=16] {'replica'}, dimensions={0} | all-to-all | bytes 6291456 | tf_op jit(solution)/shard_map/all_to_all | solution.py:129
  107.2 4.7 %reshape.34 = bf16[192,8192]{1,0:T(8,128)(2,1)} reshape(bf16[16,12,8192]{2,1,0:T(8,128)(2,1)} %all_to_all.10) | data formatting | bytes 6291456 | tf_op jit(solution)/shard_map/reshape | solution.py:132
  111.9 4.7 %fusion = bf16[192,4096]{1,0:T(8,128)(2,1)S(1)} fusion(bf16[192,8192]{1,0:T(8,128)(2,1)} %reshape.34, bf16[1,8192,64]{1,2,0:T(8,128)(2,1)} %param.20, bf16[1,64,4096]{2,1,0:T(8,128)(2,1)} %param.21), kind=kOutput, calls=%fused_computation.2 | convolution fusion | flops 303575040 | bytes 6291456 | tf_op jit(solution)/shard_map/dot_general | solution.py:137
  116.6 0.0 copy-start.4
  116.7 0.0 copy-start.5
  116.7 1.5 reshape.35
  118.2 5.7 %all-to-all-start.1 = ((bf16[16,12,4096]{2,1,0:T(8,128)(2,1)}), bf16[16,12,4096]{2,1,0:T(8,128)(2,1)}, u32[]{:S(2)}, u32[]{:S(2)}) async-start(bf16[16,12,4096]{2,1,0:T(8,128)(2,1)} %reshape.35), calls=%async_computation.1 | async-start | bytes 4194304 | tf_op jit(solution)/shard_map/all_to_all | solution.py:140
  123.8 0.0 copy-done.4
  123.9 0.0 copy-start.3
  123.9 0.1 broadcast_in_dim.20
  123.9 0.0 copy-done.5
  123.9 0.1 broadcast_in_dim.36
  124.0 47.1 %all-to-all-done.1 = bf16[16,12,4096]{2,1,0:T(8,128)(2,1)} async-done(((bf16[16,12,4096]{2,1,0:T(8,128)(2,1)}), bf16[16,12,4096]{2,1,0:T(8,128)(2,1)}, u32[]{:S(2)}, u32[]{:S(2)}) %all-to-all-start.1) | async-done | bytes 1572896 | tf_op jit(solution)/shard_map/all_to_all | solution.py:140
  171.1 3.6 %reshape.36 = bf16[192,4096]{1,0:T(8,128)(2,1)} reshape(bf16[16,12,4096]{2,1,0:T(8,128)(2,1)} %all-to-all-done.1) | data formatting | bytes 3145728 | tf_op jit(solution)/shard_map/reshape | solution.py:141
  174.7 1.8 convolution_convert_fusion.1.d_ref
  176.5 0.1 broadcast_in_dim.21.lengths_ref
  176.6 0.1 broadcast_in_dim.37.joins_ref
  176.6 0.0 copy-done.3
  176.6 0.0 copy-start.1
  176.7 1.9 copy-done.1
  178.5 0.0 copy-start.2
  178.5 1.9 copy-done.2
  180.4 0.0 copy-start.6
  180.4 12.0 %shard_map.109 = bf16[96,4096]{1,0:T(8,128)(2,1)S(1)} custom-call(s32[6,16,128]{2,1,0:T(8,128)S(1)} %broadcast_in_dim.21.lengths_ref, s32[6,16,128]{2,1,0:T(8,128)S(1)} %broadcast_in_dim.37.joins_ref, bf16[96,4096]{1,0:T(8,128)(2,1)S(1)} %copy-done.3, bf16[96,4096]{1,0:T(8,128)(2,1)S(1)} %convolution_convert_fusion.1.d_ref, bf16[3072,512]{1,0:T(8,128)(2,1)S(1)} %bitcast.14, ...), custom_call_target="tpu_custom_call" | custom-call | flops 603979776 | bytes 8650752 | tf_op jit(solution)/shard_map/pallas_call | solution.py:82
  192.5 0.9 collective-permute-start
  193.4 0.0 copy-done.6
  193.4 0.6 dynamic_slice.4
  194.7 0.7 collective-permute-done
  195.3 1.0 broadcast_select_fusion
  (1 shorter events, 0.0 us)
Async XLA Ops:
  0.0 1.4 copy-start
  116.6 7.2 %copy-start.4 = (s32[96]{0:T(128)S(1)}, s32[96]{0:T(128)}, u32[]{:S(2)}) copy-start(s32[96]{0:T(128)} %param.15) | copy-start | bytes 1156
  116.7 7.3 %copy-start.5 = (s32[96]{0:T(128)S(1)}, s32[96]{0:T(128)}, u32[]{:S(2)}) copy-start(s32[96]{0:T(128)} %param.16) | copy-start | bytes 1156
  118.2 52.9 %all-to-all-start.1 = ((bf16[16,12,4096]{2,1,0:T(8,128)(2,1)}), bf16[16,12,4096]{2,1,0:T(8,128)(2,1)}, u32[]{:S(2)}, u32[]{:S(2)}) async-start(bf16[16,12,4096]{2,1,0:T(8,128)(2,1)} %reshape.35), calls=%async_computation.1 | async-start | bytes 4194304 | tf_op jit(solution)/shard_map/all_to_all | solution.py:140
  123.9 52.8 %copy-start.3 = (bf16[96,4096]{1,0:T(8,128)(2,1)S(1)}, bf16[96,4096]{1,0:T(8,128)(2,1)}, u32[]{:S(2)}) copy-start(bf16[96,4096]{1,0:T(8,128)(2,1)} %q_ref.1) | copy-start | bytes 2359300
  176.6 1.9 copy-start.1
  178.5 1.9 copy-start.2
  180.4 13.0 %copy-start.6 = (s32[8]{0:T(128)S(1)}, s32[8]{0:T(128)}, u32[]{:S(2)}) copy-start(s32[8]{0:T(128)} %param.19) | copy-start | bytes 100
  192.5 2.9 %collective-permute-start = (bf16[96,4096]{1,0:T(8,128)(2,1)S(1)}, bf16[96,4096]{1,0:T(8,128)(2,1)S(1)}, u32[]{:S(2)}, u32[]{:S(2)}) collective-permute-start(bf16[96,4096]{1,0:T(8,128)(2,1)S(1)} %shard_map.109), channel_id=1, source_target_pairs={{0,1},{1,0},{2,3},{3,2},{4,5},{5,4},{6,7},{7,6},{8,9},{9,8},{10,11... | collective-permute-start | bytes 2359304 | tf_op jit(solution)/shard_map/ppermute | solution.py:104

commit v2 on v1

--- a/solution.py
+++ b/solution.py
@@ -13,6 +13,7 @@
 HEAD_WIDTH = 128
 SPAN = 16
 ADAPTER_SCALE = 0.5
+ADAPTER_RANK = 64
 NEG_LARGE = -1e30
 
 STEP_ROWS = 16
@@ -111,6 +112,333 @@
         jnp.where(adapter_column[:, None] == table[None, :], adapter_owner_row[None, :], 0), axis=1
     )
 
+PLANE = 4
+ROUTES = pl.DeviceIdType.MESH
+
+
+def gathered_kernel(
+    layers, h_ref, st_ref, down_ref, up_ref, out_ref,
+    h_buf, st_buf, down_buf, up_buf, part, part_in, narrow, narrow_all, spread, wide,
+    local_sem, h_send, h_recv, st_send, st_recv,
+    down_send, down_recv, up_send, up_recv, climb_send, sink_send, climb_up_send, sink_up_send,
+    part_send, part_recv, narrow_send, narrow_recv, wide_send, wide_recv,
+):
+    rows = h_ref.shape[0]
+    rank, depth = ADAPTER_RANK, down_buf.shape[1]
+    lanes = up_buf.shape[1]
+    group, here = lax.axis_index("groups"), lax.axis_index("replica")
+    layer, local = here // PLANE, here % PLANE
+    side, core = local // 2, local % 2
+    me = group * PLANE + local
+    peers = 2 * PLANE
+
+    def peer(i):
+        g = (group + i // 4) % 2
+        l = ((side + (i // 2) % 2) % 2) * 2 + (core + i % 2) % 2
+        return g, l, g * PLANE + l
+
+    def push(src, dst, send, recv, g, r):
+        return pltpu.make_async_remote_copy(
+            src_ref=src, dst_ref=dst, send_sem=send, recv_sem=recv,
+            device_id=(g, r), device_id_type=ROUTES,
+        )
+
+    def over_peers(body):
+        def step(i, carry):
+            body(*peer(i))
+            return carry
+
+        lax.fori_loop(1, peers, step, 0)
+
+    def over_locals(body, first=0):
+        def step(i, carry):
+            body(peer(i)[1])
+            return carry
+
+        lax.fori_loop(first, PLANE, step, 0)
+
+    barrier = pltpu.get_barrier_semaphore()
+
+    def greet(g, l, j):
+        pl.semaphore_signal(
+            barrier, inc=1, device_id=(g, layer * PLANE + l), device_id_type=ROUTES
+        )
+
+    over_peers(greet)
+
+    @pl.when(layer < layers - 1)
+    def _():
+        pl.semaphore_signal(barrier, inc=1, device_id=(group, here + PLANE), device_id_type=ROUTES)
+
+    @pl.when(layer > 0)
+    def _():
+        pl.semaphore_signal(barrier, inc=1, device_id=(group, here - PLANE), device_id_type=ROUTES)
+
+    inner = (layer + layers - 1) // layers - (layer + 1) // layers
+    pl.semaphore_wait(barrier, peers + inner)
+
+    def stored(buf, a):
+        return buf.at[pl.ds(a * rank, rank), :]
+
+    def piece(ref, j, size):
+        return ref.at[:, pl.ds(j * size, size)]
+
+    def block(ref, j):
+        return ref.at[pl.ds(j * rows, rows), :]
+
+    mine = [
+        pltpu.make_async_copy(piece(down_ref, me, depth), stored(down_buf, here), local_sem.at[0]),
+        pltpu.make_async_copy(piece(up_ref, me, lanes), stored(up_buf, here), local_sem.at[1]),
+        pltpu.make_async_copy(piece(h_ref, me, depth), block(h_buf, me), local_sem.at[2]),
+        pltpu.make_async_copy(st_ref, block(st_buf, me), local_sem.at[3]),
+    ]
+    for copy in mine:
+        copy.start()
+
+    def down_copy(l):
+        j = group * PLANE + l
+        return push(
+            piece(down_ref, j, depth), stored(down_buf, here),
+            down_send.at[l], down_recv.at[here], group, layer * PLANE + l,
+        )
+
+    def up_copy(l):
+        j = group * PLANE + l
+        return push(
+            piece(up_ref, j, lanes), stored(up_buf, here),
+            up_send.at[l], up_recv.at[here], group, layer * PLANE + l,
+        )
+
+    def h_copy(g, l, j):
+        return push(
+            piece(h_ref, j, depth), block(h_buf, me),
+            h_send.at[j], h_recv.at[me], g, layer * PLANE + l,
+        )
+
+    def st_copy(g, l, j):
+        return push(
+            st_ref, block(st_buf, me), st_send.at[j], st_recv.at[me], g, layer * PLANE + l
+        )
+
+    over_locals(lambda l: down_copy(l).start(), 1)
+    mine[0].wait()
+    mine[1].wait()
+
+    def onward(buf, a, send, recv, step):
+        return push(
+            stored(buf, a), stored(buf, a), send.at[a], recv.at[a], group, here + step * PLANE
+        )
+
+    def arrived(buf, a, recv):
+        push(stored(buf, a), stored(buf, a), local_sem.at[4], recv.at[a], group, here).wait_recv()
+
+    def first_hop(buf, recv, climb, sink, l):
+        a = layer * PLANE + l
+
+        @pl.when(l != local)
+        def _():
+            arrived(buf, a, recv)
+
+        @pl.when(layer < layers - 1)
+        def _():
+            onward(buf, a, climb, recv, 1).start()
+
+        @pl.when(layer > 0)
+        def _():
+            onward(buf, a, sink, recv, -1).start()
+
+    def later_hop(buf, recv, climb, sink, t, l):
+        @pl.when(layer - t >= 0)
+        def _():
+            a = (layer - t) * PLANE + l
+            arrived(buf, a, recv)
+
+            @pl.when(layer < layers - 1)
+            def _():
+                onward(buf, a, climb, recv, 1).start()
+
+        @pl.when(layer + t < layers)
+        def _():
+            a = (layer + t) * PLANE + l
+            arrived(buf, a, recv)
+
+            @pl.when(layer > 0)
+            def _():
+                onward(buf, a, sink, recv, -1).start()
+
+    downs = (down_buf, down_recv, climb_send, sink_send)
+    ups = (up_buf, up_recv, climb_up_send, sink_up_send)
+    first_hop(*downs, local)
+    over_peers(lambda g, l, j: st_copy(g, l, j).start())
+    over_locals(lambda l: first_hop(*downs, l), 1)
+    over_peers(lambda g, l, j: h_copy(g, l, j).start())
+    over_locals(lambda l: up_copy(l).start(), 1)
+    for t in range(1, layers - 1):
+        over_locals(lambda l: later_hop(*downs, t, l))
+    over_locals(lambda l: first_hop(*ups, l))
+    mine[2].wait()
+    mine[3].wait()
+
+    def here_recv(src, dst, recv, g, l):
+        push(src, dst, local_sem.at[4], recv, g, layer * PLANE + l).wait_recv()
+
+    over_peers(lambda g, l, j: here_recv(block(h_buf, j), block(h_buf, j), h_recv.at[j], g, l))
+    over_peers(lambda g, l, j: here_recv(block(st_buf, j), block(st_buf, j), st_recv.at[j], g, l))
+    over_locals(lambda l: later_hop(*downs, layers - 1, l))
+
+    lane = lax.broadcasted_iota(jnp.int32, (1, 2 * rank), 1) // rank
+    part[...] = jnp.zeros_like(part)
+
+    def narrowed(s, carry):
+        at = pl.ds(s * 4 * rank, 4 * rank)
+        both = lax.dot_general(
+            h_buf[...], down_buf[at, :], (((1,), (1,)), ((), ())),
+            preferred_element_type=jnp.float32,
+        )
+        stores = st_buf[...]
+        kept = jnp.where(stores == s * 4 + lane, both[:, : 2 * rank], 0.0)
+        kept = kept + jnp.where(stores == s * 4 + 2 + lane, both[:, 2 * rank :], 0.0)
+        part[...] += kept
+        return carry
+
+    lax.fori_loop(0, down_buf.shape[0] // (4 * rank), narrowed, 0)
+
+    def part_copy(g, l, j):
+        return push(
+            block(part, j), part_in.at[me], part_send.at[j], part_recv.at[me],
+            g, layer * PLANE + l,
+        )
+
+    over_peers(lambda g, l, j: part_copy(g, l, j).start())
+    for t in range(1, layers - 1):
+        over_locals(lambda l: later_hop(*ups, t, l))
+    over_peers(lambda g, l, j: here_recv(part_in.at[j], part_in.at[j], part_recv.at[j], g, l))
+    part_in[me] = part[pl.ds(me * rows, rows), :]
+    total = part_in[0]
+    for j in range(1, peers):
+        total = total + part_in[j]
+    total = total + pltpu.roll(total, rank, 1)
+    narrow[...] = total.astype(jnp.bfloat16)
+
+    def narrow_copy(g, l, j):
+        return push(
+            narrow, block(narrow_all, me), narrow_send.at[j], narrow_recv.at[me],
+            g, layer * PLANE + l,
+        )
+
+    over_peers(lambda g, l, j: narrow_copy(g, l, j).start())
+    narrow_all[pl.ds(me * rows, rows), :] = narrow[...]
+    over_peers(
+        lambda g, l, j: here_recv(block(narrow_all, j), block(narrow_all, j), narrow_recv.at[j], g, l)
+    )
+    for s in range(spread.shape[1] // (2 * rank)):
+        spread[:, s * 2 * rank : (s + 1) * 2 * rank] = jnp.where(
+            st_buf[...] == 2 * s + lane, narrow_all[...].astype(jnp.float32), 0.0
+        ).astype(jnp.bfloat16)
+    over_locals(lambda l: later_hop(*ups, layers - 1, l))
+
+    def widened(c, carry):
+        at = pl.ds(c * 256, 256)
+        block_of = jnp.dot(spread[...], up_buf[:, at], preferred_element_type=jnp.float32)
+        wide[:, at] = (ADAPTER_SCALE * block_of).astype(jnp.bfloat16)
+        return carry
+
+    lax.fori_loop(0, lanes // 256, widened, 0)
+
+    def wide_copy(g, l, j):
+        return push(
+            block(wide, j), piece(out_ref, me, lanes), wide_send.at[j], wide_recv.at[me],
+            g, layer * PLANE + l,
+        )
+
+    over_peers(lambda g, l, j: wide_copy(g, l, j).start())
+    last = pltpu.make_async_copy(block(wide, me), piece(out_ref, me, lanes), local_sem.at[5])
+    last.start()
+    last.wait()
+    over_peers(
+        lambda g, l, j: here_recv(
+            piece(out_ref, j, lanes), piece(out_ref, j, lanes), wide_recv.at[j], g, l
+        )
+    )
+
+    def left(l):
+        down_copy(l).wait_send()
+        up_copy(l).wait_send()
+
+    over_locals(left, 1)
+
+    def left_peer(g, l, j):
+        h_copy(g, l, j).wait_send()
+        st_copy(g, l, j).wait_send()
+        part_copy(g, l, j).wait_send()
+        narrow_copy(g, l, j).wait_send()
+        wide_copy(g, l, j).wait_send()
+
+    over_peers(left_peer)
+
+    def passed(s, carry):
+        def one(l):
+            a = s * PLANE + l
+
+            @pl.when((layer < layers - 1) & (s <= layer))
+            def _():
+                onward(down_buf, a, climb_send, down_recv, 1).wait_send()
+                onward(up_buf, a, climb_up_send, up_recv, 1).wait_send()
+
+            @pl.when((layer > 0) & (s >= layer))
+            def _():
+                onward(down_buf, a, sink_send, down_recv, -1).wait_send()
+                onward(up_buf, a, sink_up_send, up_recv, -1).wait_send()
+
+        over_locals(one)
+        return carry
+
+    lax.fori_loop(0, layers, passed, 0)
+
+
+def gathered_rows(hidden_state_rows, stores, down_factors, up_factors):
+    replicas = lax.axis_size("replica")
+    rows, depth = hidden_state_rows.shape
+    rank, width = up_factors.shape[1:]
+    layers = replicas // PLANE
+    peers = 2 * PLANE
+    down = jnp.swapaxes(down_factors[0], 0, 1)
+    tags = jnp.broadcast_to(stores[:, None], (rows, 128))
+    dma = pltpu.SemaphoreType.DMA
+    here = pl.BlockSpec(memory_space=pltpu.VMEM)
+    return pl.pallas_call(
+        functools.partial(gathered_kernel, layers),
+        in_specs=[here] * 4,
+        out_specs=pl.BlockSpec(memory_space=pl.ANY),
+        out_shape=jax.ShapeDtypeStruct((rows, width), jnp.bfloat16),
+        scratch_shapes=[
+            pltpu.VMEM((peers * rows, depth // peers), jnp.bfloat16),
+            pltpu.VMEM((peers * rows, 128), jnp.int32),
+            pltpu.VMEM((replicas * rank, depth // peers), jnp.bfloat16),
+            pltpu.VMEM((replicas * rank, width // peers), jnp.bfloat16),
+            pltpu.VMEM((peers * rows, 128), jnp.float32),
+            pltpu.VMEM((peers, rows, 128), jnp.float32),
+            pltpu.VMEM((rows, 128), jnp.bfloat16),
+            pltpu.VMEM((peers * rows, 128), jnp.bfloat16),
+            pltpu.VMEM((peers * rows, replicas * rank), jnp.bfloat16),
+            pltpu.VMEM((peers * rows, width // peers), jnp.bfloat16),
+            dma((6,)),
+            dma((peers,)), dma((peers,)), dma((peers,)), dma((peers,)),
+            dma((PLANE,)), dma((replicas,)), dma((PLANE,)), dma((replicas,)),
+            dma((replicas,)), dma((replicas,)), dma((replicas,)), dma((replicas,)),
+            dma((peers,)), dma((peers,)), dma((peers,)), dma((peers,)),
+            dma((peers,)), dma((peers,)),
+        ],
+        compiler_params=pltpu.CompilerParams(
+            collective_id=0, has_side_effects=True, vmem_limit_bytes=40 * 1024 * 1024
+        ),
+        cost_estimate=pl.CostEstimate(
+            flops=2 * peers * rows * replicas * rank * (depth + width) // peers,
+            bytes_accessed=2 * rows * (depth + width) + 2 * rank * (depth + width),
+            transcendentals=0,
+        ),
+    )(hidden_state_rows, tags, down, up_factors[0])
+
 
 def routed_rows(hidden_state_rows, stores, down_factors, up_factors):
     replicas = lax.axis_size("replica")
@@ -159,7 +487,9 @@
     here = lax.axis_index("replica")
     trade = lax.dynamic_index_in_dim(pair_trade_flags, here // 2, 0, keepdims=False) == 1
     stores = stores_of(adapter_index, adapter_owner_row)
-    query_shift = routed_rows(hidden_state_rows, stores, down_factors, up_factors)
+    few = lax.axis_size("replica") == 4 * PLANE and lax.axis_size("groups") == 2
+    shifted = gathered_rows if few else routed_rows
+    query_shift = shifted(hidden_state_rows, stores, down_factors, up_factors)
     attended = attend(
         base_queries,
         query_shift,

time: 197 us -> 92.5 us (0.47)
  the two profiles are of different devices: /device:TPU:17 before, /device:TPU:0 now
where the time goes in v2:
time: 92.5 us; the launch traced here: 92.2 us
  Pallas kernels  82.6 us (89%)
  local copies, waits for them, and re-layouts  5.97 us (6%)
  other arithmetic  1.72 us (2%)
    pallas_call x1, Pallas kernels, gathered_rows(): pl.pallas_call(functools.partial(gathered_kernel, layers), in_specs=[here...  70.6 us
    pallas_call x1, Pallas kernels, attend(): pl.pallas_call(attend_kernel, grid=(steps,), in_specs=[small, small, wide...  12 us
    unnamed x14, local copies, waits for them, and re-layouts  3.7 us
  transfers between devices with their start and end apart: 1, of which 1 were waited for; matrix products, arithmetic and copies ran while one was open for 1% of the time, Pallas kernels for 0%

profile of v2, /device:TPU:0, one launch (start us, length us, event | category | flops | bytes accessed | tf_op | source)
XLA Modules:
  0.0 92.2 jit_solution(17127896054202010804)
XLA Ops:
  0.0 0.7 broadcast_in_dim.34
  0.7 0.7 broadcast_in_dim.36
  1.5 0.8 select_reduce_fusion
  2.2 0.1 broadcast_in_dim.40.st_ref
  2.3 0.0 copy-start.3
  2.3 1.4 %copy-done.3 = bf16[96,8192]{1,0:T(8,128)(2,1)S(1)} copy-done((bf16[96,8192]{1,0:T(8,128)(2,1)S(1)}, bf16[96,8192]{1,0:T(8,128)(2,1)}, u32[]{:S(2)}) %copy-start.3) | copy-done | bytes 1572888
  3.7 0.0 copy-start.4
  3.7 1.2 %copy-done.4 = bf16[1,8192,64]{1,2,0:T(8,128)(2,1)S(1)} copy-done((bf16[1,8192,64]{1,2,0:T(8,128)(2,1)S(1)}, bf16[1,8192,64]{1,2,0:T(8,128)(2,1)}, u32[]{:S(2)}) %copy-start.4) | copy-done | bytes 1048600
  4.9 0.0 copy-start.5
  4.9 1.0 %copy-done.5 = bf16[1,64,4096]{2,1,0:T(8,128)(2,1)S(1)} copy-done((bf16[1,64,4096]{2,1,0:T(8,128)(2,1)S(1)}, bf16[1,64,4096]{2,1,0:T(8,128)(2,1)}, u32[]{:S(2)}) %copy-start.5) | copy-done | bytes 524312
  6.0 0.0 copy-start
  6.0 0.0 copy-start.1
  6.0 0.0 copy-start.2
  6.0 70.6 %shard_map.109.d_ref = bf16[96,4096]{1,0:T(8,128)(2,1)S(1)} custom-call(bf16[96,8192]{1,0:T(8,128)(2,1)S(1)} %copy-done.3, s32[96,128]{1,0:T(8,128)S(1)} %broadcast_in_dim.40.st_ref, bf16[64,8192]{1,0:T(8,128)(2,1)S(1)} %bitcast.10, bf16[64,4096]{1,0:T(8,128)(2,1)S(1)} %bitcast.11), custom_call_target="tpu_custom_call" | custom-call | flops 2415919104 | bytes 3932160 | tf_op jit(solution)/shard_map/pallas_call | solution.py:409
  76.6 0.1 broadcast_in_dim.35.lengths_ref
  76.7 0.1 broadcast_in_dim.37.joins_ref
  76.7 0.0 copy-done
  76.7 0.0 copy-done.1
  76.8 0.0 copy-done.2
  76.8 0.0 copy-start.6
  76.8 12.0 %shard_map.110 = bf16[96,4096]{1,0:T(8,128)(2,1)S(1)} custom-call(s32[6,16,128]{2,1,0:T(8,128)S(1)} %broadcast_in_dim.35.lengths_ref, s32[6,16,128]{2,1,0:T(8,128)S(1)} %broadcast_in_dim.37.joins_ref, bf16[96,4096]{1,0:T(8,128)(2,1)S(1)} %copy-done.2, bf16[96,4096]{1,0:T(8,128)(2,1)S(1)} %shard_map.109.d_ref, bf16[3072,512]{1,0:T(8,128)(2,1)S(1)} %bitcast.8, ...), custom_call_target="tpu_custom_call" | custom-call | flops 603979776 | bytes 8650752 | tf_op jit(solution)/shard_map/pallas_call | solution.py:83
  88.8 0.5 collective-permute-start
  89.4 0.0 copy-done.6
  89.4 0.6 dynamic_slice.4
  90.6 0.7 collective-permute-done
  91.3 1.0 %broadcast_select_fusion = bf16[96,4096]{1,0:T(8,128)(2,1)} fusion(bf16[96,4096]{1,0:T(8,128)(2,1)S(1)} %collective-permute-done, bf16[96,4096]{1,0:T(8,128)(2,1)S(1)} %shard_map.110, pred[]{:T(512)} %bitcast), kind=kLoop, calls=%fused_computation | loop fusion | flops 393216 | bytes 2359297 | tf_op jit(solution)/shard_map/jit(_where)/select_n | solution.py:501
Async XLA Ops:
  2.3 1.4 %copy-start.3 = (bf16[96,8192]{1,0:T(8,128)(2,1)S(1)}, bf16[96,8192]{1,0:T(8,128)(2,1)}, u32[]{:S(2)}) copy-start(bf16[96,8192]{1,0:T(8,128)(2,1)} %h_ref.1) | copy-start | bytes 4718596
  3.7 1.2 %copy-start.4 = (bf16[1,8192,64]{1,2,0:T(8,128)(2,1)S(1)}, bf16[1,8192,64]{1,2,0:T(8,128)(2,1)}, u32[]{:S(2)}) copy-start(bf16[1,8192,64]{1,2,0:T(8,128)(2,1)} %param.20) | copy-start | bytes 3145732
  4.9 1.0 %copy-start.5 = (bf16[1,64,4096]{2,1,0:T(8,128)(2,1)S(1)}, bf16[1,64,4096]{2,1,0:T(8,128)(2,1)}, u32[]{:S(2)}) copy-start(bf16[1,64,4096]{2,1,0:T(8,128)(2,1)} %param.21) | copy-start | bytes 1572868
  6.0 70.8 %copy-start = (bf16[96,32,512]{2,1,0:T(8,128)(2,1)S(1)}, bf16[96,32,512]{2,1,0:T(8,128)(2,1)}, u32[]{:S(2)}) copy-start(bf16[96,32,512]{2,1,0:T(8,128)(2,1)} %param.13) | copy-start | bytes 9437188
  6.0 70.8 %copy-start.1 = (bf16[96,32,512]{2,1,0:T(8,128)(2,1)S(1)}, bf16[96,32,512]{2,1,0:T(8,128)(2,1)}, u32[]{:S(2)}) copy-start(bf16[96,32,512]{2,1,0:T(8,128)(2,1)} %param.14) | copy-start | bytes 9437188
  6.0 70.8 %copy-start.2 = (bf16[96,4096]{1,0:T(8,128)(2,1)S(1)}, bf16[96,4096]{1,0:T(8,128)(2,1)}, u32[]{:S(2)}) copy-start(bf16[96,4096]{1,0:T(8,128)(2,1)} %q_ref.1) | copy-start | bytes 2359300
  76.8 12.6 %copy-start.6 = (s32[8]{0:T(128)S(1)}, s32[8]{0:T(128)}, u32[]{:S(2)}) copy-start(s32[8]{0:T(128)} %param.19) | copy-start | bytes 100
  88.8 2.4 %collective-permute-start = (bf16[96,4096]{1,0:T(8,128)(2,1)S(1)}, bf16[96,4096]{1,0:T(8,128)(2,1)S(1)}, u32[]{:S(2)}, u32[]{:S(2)}) collective-permute-start(bf16[96,4096]{1,0:T(8,128)(2,1)S(1)} %shard_map.110), channel_id=1, source_target_pairs={{0,1},{1,0},{2,3},{3,2},{4,5},{5,4},{6,7},{7,6},{8,9},{9,8},{10,11... | collective-permute-start | bytes 2359304 | tf_op jit(solution)/shard_map/ppermute | solution.py:105

commit v3 on v2

--- a/solution.py
+++ b/solution.py
@@ -118,8 +118,9 @@
 
 def gathered_kernel(
     layers, h_ref, st_ref, down_ref, up_ref, out_ref,
-    h_buf, st_buf, down_buf, up_buf, part, part_in, narrow, narrow_all, spread, wide,
+    h_buf, far_buf, st_buf, far_st, tags, far_tags, down_buf, up_buf, part, packed, far_packed, part_in, total_ref, narrow, narrow_all, spread, wide,
     local_sem, h_send, h_recv, st_send, st_recv,
+    far_send, far_recv, far_st_send, far_st_recv, far_part_send, far_part_recv,
     down_send, down_recv, up_send, up_recv, climb_send, sink_send, climb_up_send, sink_up_send,
     part_send, part_recv, narrow_send, narrow_recv, wide_send, wide_recv,
 ):
@@ -131,6 +132,10 @@
     side, core = local // 2, local % 2
     me = group * PLANE + local
     peers = 2 * PLANE
+    half, packs = depth // 2, rows // 2
+    partner = layer + 1 - 2 * (layer % 2)
+    end = (layer == 0) | (layer == layers - 1)
+    inside = (layer > 0) & (layer < layers - 1)
 
     def peer(i):
         g = (group + i // 4) % 2
@@ -150,6 +155,13 @@
 
         lax.fori_loop(1, peers, step, 0)
 
+    def over_all(body):
+        def step(i, carry):
+            body(*peer(i))
+            return carry
+
+        lax.fori_loop(0, peers, step, 0)
+
     def over_locals(body, first=0):
         def step(i, carry):
             body(peer(i)[1])
@@ -166,19 +178,38 @@
 
     over_peers(greet)
 
-    @pl.when(layer < layers - 1)
-    def _():
-        pl.semaphore_signal(barrier, inc=1, device_id=(group, here + PLANE), device_id_type=ROUTES)
-
-    @pl.when(layer > 0)
-    def _():
-        pl.semaphore_signal(barrier, inc=1, device_id=(group, here - PLANE), device_id_type=ROUTES)
+    def greet_far(g, l, j):
+        pl.semaphore_signal(
+            barrier, inc=1, device_id=(g, partner * PLANE + l), device_id_type=ROUTES
+        )
+
+    over_all(greet_far)
+
+    @pl.when(inside)
+    def _():
+        other = (2 * layer - partner) * PLANE + local
+        pl.semaphore_signal(barrier, inc=1, device_id=(group, other), device_id_type=ROUTES)
 
     inner = (layer + layers - 1) // layers - (layer + 1) // layers
-    pl.semaphore_wait(barrier, peers + inner)
+    pl.semaphore_wait(barrier, 2 * peers - 1 + inner)
 
     def stored(buf, a):
         return buf.at[pl.ds(a * rank, rank), :]
+
+    def stored_half(buf, a):
+        return buf.at[pl.ds(a * rank, rank), pl.ds(0, half)]
+
+    def left_half(ref, j):
+        return ref.at[:, pl.ds(j * depth, half)]
+
+    def right_half(ref, j):
+        return ref.at[:, pl.ds(j * depth + half, half)]
+
+    def near_half(j):
+        return h_buf.at[pl.ds(j * rows, rows), pl.ds(0, half)]
+
+    def tag_rows(ref, j):
+        return ref.at[pl.ds(j * 8, 8), :]
 
     def piece(ref, j, size):
         return ref.at[:, pl.ds(j * size, size)]
@@ -190,7 +221,7 @@
         pltpu.make_async_copy(piece(down_ref, me, depth), stored(down_buf, here), local_sem.at[0]),
         pltpu.make_async_copy(piece(up_ref, me, lanes), stored(up_buf, here), local_sem.at[1]),
         pltpu.make_async_copy(piece(h_ref, me, depth), block(h_buf, me), local_sem.at[2]),
-        pltpu.make_async_copy(st_ref, block(st_buf, me), local_sem.at[3]),
+        pltpu.make_async_copy(st_ref, tag_rows(st_buf, me), local_sem.at[3]),
     ]
     for copy in mine:
         copy.start()
@@ -215,63 +246,120 @@
             h_send.at[j], h_recv.at[me], g, layer * PLANE + l,
         )
 
+    def h_half(g, l, j):
+        return push(
+            left_half(h_ref, j), near_half(me), h_send.at[j], h_recv.at[me], g, layer * PLANE + l
+        )
+
+    def far_copy(g, l, j):
+        return push(
+            right_half(h_ref, j), block(far_buf, me), far_send.at[j], far_recv.at[me],
+            g, partner * PLANE + l,
+        )
+
     def st_copy(g, l, j):
         return push(
-            st_ref, block(st_buf, me), st_send.at[j], st_recv.at[me], g, layer * PLANE + l
+            st_ref, tag_rows(st_buf, me), st_send.at[j], st_recv.at[me], g, layer * PLANE + l
+        )
+
+    def far_st_copy(g, l, j):
+        return push(
+            st_ref, tag_rows(far_st, me), far_st_send.at[j], far_st_recv.at[me],
+            g, partner * PLANE + l,
         )
 
     over_locals(lambda l: down_copy(l).start(), 1)
     mine[0].wait()
     mine[1].wait()
 
-    def onward(buf, a, send, recv, step):
-        return push(
-            stored(buf, a), stored(buf, a), send.at[a], recv.at[a], group, here + step * PLANE
-        )
-
-    def arrived(buf, a, recv):
-        push(stored(buf, a), stored(buf, a), local_sem.at[4], recv.at[a], group, here).wait_recv()
-
-    def first_hop(buf, recv, climb, sink, l):
+    def onward(buf, a, send, recv, step, view):
+        return push(
+            view(buf, a), view(buf, a), send.at[a], recv.at[a], group, here + step * PLANE
+        )
+
+    def arrived(buf, a, recv, view):
+        push(view(buf, a), view(buf, a), local_sem.at[4], recv.at[a], group, here).wait_recv()
+
+    def hop(buf, a, send, recv, step, split, do):
+        if not split:
+            do(onward(buf, a, send, recv, step, stored))
+            return
+        to_end = layer == (layers - 2 if step > 0 else 1)
+
+        @pl.when(to_end)
+        def _():
+            do(onward(buf, a, send, recv, step, stored_half))
+
+        @pl.when(jnp.logical_not(to_end))
+        def _():
+            do(onward(buf, a, send, recv, step, stored))
+
+    def start(copy):
+        copy.start()
+
+    def first_hop(buf, recv, climb, sink, split, l):
         a = layer * PLANE + l
 
         @pl.when(l != local)
         def _():
-            arrived(buf, a, recv)
+            arrived(buf, a, recv, stored)
 
         @pl.when(layer < layers - 1)
         def _():
-            onward(buf, a, climb, recv, 1).start()
+            hop(buf, a, climb, recv, 1, split, start)
 
         @pl.when(layer > 0)
         def _():
-            onward(buf, a, sink, recv, -1).start()
-
-    def later_hop(buf, recv, climb, sink, t, l):
+            hop(buf, a, sink, recv, -1, split, start)
+
+    def landed(buf, a, recv, split):
+        if not split:
+            arrived(buf, a, recv, stored)
+            return
+
+        @pl.when(end)
+        def _():
+            arrived(buf, a, recv, stored_half)
+
+        @pl.when(inside)
+        def _():
+            arrived(buf, a, recv, stored)
+
+    def later_hop(buf, recv, climb, sink, split, t, l):
         @pl.when(layer - t >= 0)
         def _():
             a = (layer - t) * PLANE + l
-            arrived(buf, a, recv)
+            landed(buf, a, recv, split)
 
             @pl.when(layer < layers - 1)
             def _():
-                onward(buf, a, climb, recv, 1).start()
+                hop(buf, a, climb, recv, 1, split, start)
 
         @pl.when(layer + t < layers)
         def _():
             a = (layer + t) * PLANE + l
-            arrived(buf, a, recv)
+            landed(buf, a, recv, split)
 
             @pl.when(layer > 0)
             def _():
-                onward(buf, a, sink, recv, -1).start()
-
-    downs = (down_buf, down_recv, climb_send, sink_send)
-    ups = (up_buf, up_recv, climb_up_send, sink_up_send)
+                hop(buf, a, sink, recv, -1, split, start)
+
+    downs = (down_buf, down_recv, climb_send, sink_send, True)
+    ups = (up_buf, up_recv, climb_up_send, sink_up_send, False)
     first_hop(*downs, local)
     over_peers(lambda g, l, j: st_copy(g, l, j).start())
     over_locals(lambda l: first_hop(*downs, l), 1)
-    over_peers(lambda g, l, j: h_copy(g, l, j).start())
+
+    @pl.when(end)
+    def _():
+        over_all(lambda g, l, j: far_st_copy(g, l, j).start())
+        over_all(lambda g, l, j: far_copy(g, l, j).start())
+        over_peers(lambda g, l, j: h_half(g, l, j).start())
+
+    @pl.when(inside)
+    def _():
+        over_peers(lambda g, l, j: h_copy(g, l, j).start())
+
     over_locals(lambda l: up_copy(l).start(), 1)
     for t in range(1, layers - 1):
         over_locals(lambda l: later_hop(*downs, t, l))
@@ -282,59 +370,121 @@
     def here_recv(src, dst, recv, g, l):
         push(src, dst, local_sem.at[4], recv, g, layer * PLANE + l).wait_recv()
 
-    over_peers(lambda g, l, j: here_recv(block(h_buf, j), block(h_buf, j), h_recv.at[j], g, l))
-    over_peers(lambda g, l, j: here_recv(block(st_buf, j), block(st_buf, j), st_recv.at[j], g, l))
+    def taken(view, recv):
+        return lambda g, l, j: here_recv(view(j), view(j), recv.at[j], g, l)
+
+    def tagged(src, dst):
+        for j in range(peers):
+            row = src[j * 8 : j * 8 + 1, :].astype(jnp.float32)
+            turned = jnp.transpose(jnp.broadcast_to(row, (128, 128)))
+            dst[j * rows : (j + 1) * rows, :] = turned[:rows].astype(jnp.int32)
+
+    over_peers(taken(lambda j: tag_rows(st_buf, j), st_recv))
+    tagged(st_buf, tags)
+
+    @pl.when(end)
+    def _():
+        over_peers(taken(near_half, h_recv))
+
+    @pl.when(inside)
+    def _():
+        over_peers(taken(lambda j: block(h_buf, j), h_recv))
+        over_all(taken(lambda j: tag_rows(far_st, j), far_st_recv))
+        tagged(far_st, far_tags)
+
     over_locals(lambda l: later_hop(*downs, layers - 1, l))
 
     lane = lax.broadcasted_iota(jnp.int32, (1, 2 * rank), 1) // rank
-    part[...] = jnp.zeros_like(part)
-
-    def narrowed(s, carry):
-        at = pl.ds(s * 4 * rank, 4 * rank)
-        both = lax.dot_general(
-            h_buf[...], down_buf[at, :], (((1,), (1,)), ((), ())),
-            preferred_element_type=jnp.float32,
-        )
-        stores = st_buf[...]
-        kept = jnp.where(stores == s * 4 + lane, both[:, : 2 * rank], 0.0)
-        kept = kept + jnp.where(stores == s * 4 + 2 + lane, both[:, 2 * rank :], 0.0)
-        part[...] += kept
-        return carry
-
-    lax.fori_loop(0, down_buf.shape[0] // (4 * rank), narrowed, 0)
+
+    def products(left, right, stores_ref, to):
+        part[...] = jnp.zeros_like(part)
+
+        def narrowed(s, carry):
+            at = pl.ds(s * 4 * rank, 4 * rank)
+            both = lax.dot_general(
+                left[...], right[at, :], (((1,), (1,)), ((), ())),
+                preferred_element_type=jnp.float32,
+            )
+            stores = stores_ref[...]
+            kept = jnp.where(stores == s * 4 + lane, both[:, : 2 * rank], 0.0)
+            kept = kept + jnp.where(stores == s * 4 + 2 + lane, both[:, 2 * rank :], 0.0)
+            part[...] += kept
+            return carry
+
+        lax.fori_loop(0, down_buf.shape[0] // (4 * rank), narrowed, 0)
+        summed = part[...]
+        summed = summed + pltpu.roll(summed, rank, 1)
+        for j in range(peers):
+            first = summed[j * rows : j * rows + packs]
+            second = summed[j * rows + packs : (j + 1) * rows]
+            to[j * packs : (j + 1) * packs, :] = jnp.where(lane == 0, first, second)
+
+    def packs_of(ref, j):
+        return ref.at[pl.ds(j * packs, packs), :]
 
     def part_copy(g, l, j):
         return push(
-            block(part, j), part_in.at[me], part_send.at[j], part_recv.at[me],
+            packs_of(packed, j), part_in.at[me], part_send.at[j], part_recv.at[me],
             g, layer * PLANE + l,
         )
+
+    def far_part_copy(g, l, j):
+        return push(
+            packs_of(far_packed, j), part_in.at[peers + me],
+            far_part_send.at[j], far_part_recv.at[me], g, partner * PLANE + l,
+        )
+
+    @pl.when(end)
+    def _():
+        products(h_buf.at[:, pl.ds(0, half)], down_buf.at[:, pl.ds(0, half)], tags, packed)
+
+    @pl.when(inside)
+    def _():
+        over_all(taken(lambda j: block(far_buf, j), far_recv))
+        products(far_buf, down_buf.at[:, pl.ds(half, half)], far_tags, far_packed)
+        over_all(lambda g, l, j: far_part_copy(g, l, j).start())
+        products(h_buf, down_buf, tags, packed)
 
     over_peers(lambda g, l, j: part_copy(g, l, j).start())
     for t in range(1, layers - 1):
         over_locals(lambda l: later_hop(*ups, t, l))
-    over_peers(lambda g, l, j: here_recv(part_in.at[j], part_in.at[j], part_recv.at[j], g, l))
-    part_in[me] = part[pl.ds(me * rows, rows), :]
+    over_peers(taken(lambda j: part_in.at[j], part_recv))
+    part_in[me] = packed[pl.ds(me * packs, packs), :]
     total = part_in[0]
     for j in range(1, peers):
         total = total + part_in[j]
-    total = total + pltpu.roll(total, rank, 1)
-    narrow[...] = total.astype(jnp.bfloat16)
+    total_ref[...] = total
+
+    @pl.when(end)
+    def _():
+        over_all(taken(lambda j: part_in.at[peers + j], far_part_recv))
+        more = total_ref[...]
+        for j in range(peers):
+            more = more + part_in[peers + j]
+        total_ref[...] = more
+
+    narrow[...] = total_ref[...].astype(jnp.bfloat16)
 
     def narrow_copy(g, l, j):
         return push(
-            narrow, block(narrow_all, me), narrow_send.at[j], narrow_recv.at[me],
+            narrow, packs_of(narrow_all, me), narrow_send.at[j], narrow_recv.at[me],
             g, layer * PLANE + l,
         )
 
     over_peers(lambda g, l, j: narrow_copy(g, l, j).start())
-    narrow_all[pl.ds(me * rows, rows), :] = narrow[...]
-    over_peers(
-        lambda g, l, j: here_recv(block(narrow_all, j), block(narrow_all, j), narrow_recv.at[j], g, l)
-    )
-    for s in range(spread.shape[1] // (2 * rank)):
-        spread[:, s * 2 * rank : (s + 1) * 2 * rank] = jnp.where(
-            st_buf[...] == 2 * s + lane, narrow_all[...].astype(jnp.float32), 0.0
-        ).astype(jnp.bfloat16)
+    narrow_all[pl.ds(me * packs, packs), :] = narrow[...]
+    over_peers(taken(lambda j: packs_of(narrow_all, j), narrow_recv))
+    for j in range(peers):
+        pair = narrow_all[j * packs : (j + 1) * packs, :].astype(jnp.float32)
+        turned = pltpu.roll(pair, rank, 1)
+        own = jnp.concatenate(
+            [jnp.where(lane == 0, pair, turned), jnp.where(lane == 0, turned, pair)], axis=0
+        )
+        stores = tags[j * rows : (j + 1) * rows, :]
+        for s in range(spread.shape[1] // (2 * rank)):
+            spread[j * rows : (j + 1) * rows, s * 2 * rank : (s + 1) * 2 * rank] = jnp.where(
+                stores == 2 * s + lane, own, 0.0
+            ).astype(jnp.bfloat16)
     over_locals(lambda l: later_hop(*ups, layers - 1, l))
 
     def widened(c, carry):
@@ -368,7 +518,6 @@
     over_locals(left, 1)
 
     def left_peer(g, l, j):
-        h_copy(g, l, j).wait_send()
         st_copy(g, l, j).wait_send()
         part_copy(g, l, j).wait_send()
         narrow_copy(g, l, j).wait_send()
@@ -376,19 +525,36 @@
 
     over_peers(left_peer)
 
+    def left_far(g, l, j):
+        far_st_copy(g, l, j).wait_send()
+        far_copy(g, l, j).wait_send()
+
+    @pl.when(end)
+    def _():
+        over_peers(lambda g, l, j: h_half(g, l, j).wait_send())
+        over_all(left_far)
+
+    @pl.when(inside)
+    def _():
+        over_peers(lambda g, l, j: h_copy(g, l, j).wait_send())
+        over_all(lambda g, l, j: far_part_copy(g, l, j).wait_send())
+
+    def sent(copy):
+        copy.wait_send()
+
     def passed(s, carry):
         def one(l):
             a = s * PLANE + l
 
             @pl.when((layer < layers - 1) & (s <= layer))
             def _():
-                onward(down_buf, a, climb_send, down_recv, 1).wait_send()
-                onward(up_buf, a, climb_up_send, up_recv, 1).wait_send()
+                hop(down_buf, a, climb_send, down_recv, 1, True, sent)
+                hop(up_buf, a, climb_up_send, up_recv, 1, False, sent)
 
             @pl.when((layer > 0) & (s >= layer))
             def _():
-                onward(down_buf, a, sink_send, down_recv, -1).wait_send()
-                onward(up_buf, a, sink_up_send, up_recv, -1).wait_send()
+                hop(down_buf, a, sink_send, down_recv, -1, True, sent)
+                hop(up_buf, a, sink_up_send, up_recv, -1, False, sent)
 
         over_locals(one)
         return carry
@@ -403,27 +569,36 @@
     layers = replicas // PLANE
     peers = 2 * PLANE
     down = jnp.swapaxes(down_factors[0], 0, 1)
-    tags = jnp.broadcast_to(stores[:, None], (rows, 128))
+    tags = jnp.broadcast_to(jnp.pad(stores, (0, 128 - rows))[None, :], (8, 128))
     dma = pltpu.SemaphoreType.DMA
     here = pl.BlockSpec(memory_space=pltpu.VMEM)
+    far = pl.BlockSpec(memory_space=pl.ANY)
     return pl.pallas_call(
         functools.partial(gathered_kernel, layers),
-        in_specs=[here] * 4,
+        in_specs=[far, here, far, far],
         out_specs=pl.BlockSpec(memory_space=pl.ANY),
         out_shape=jax.ShapeDtypeStruct((rows, width), jnp.bfloat16),
         scratch_shapes=[
             pltpu.VMEM((peers * rows, depth // peers), jnp.bfloat16),
+            pltpu.VMEM((peers * rows, depth // peers // 2), jnp.bfloat16),
+            pltpu.VMEM((peers * 8, 128), jnp.int32),
+            pltpu.VMEM((peers * 8, 128), jnp.int32),
+            pltpu.VMEM((peers * rows, 128), jnp.int32),
             pltpu.VMEM((peers * rows, 128), jnp.int32),
             pltpu.VMEM((replicas * rank, depth // peers), jnp.bfloat16),
             pltpu.VMEM((replicas * rank, width // peers), jnp.bfloat16),
             pltpu.VMEM((peers * rows, 128), jnp.float32),
-            pltpu.VMEM((peers, rows, 128), jnp.float32),
-            pltpu.VMEM((rows, 128), jnp.bfloat16),
-            pltpu.VMEM((peers * rows, 128), jnp.bfloat16),
+            pltpu.VMEM((peers * rows // 2, 128), jnp.float32),
+            pltpu.VMEM((peers * rows // 2, 128), jnp.float32),
+            pltpu.VMEM((2 * peers, rows // 2, 128), jnp.float32),
+            pltpu.VMEM((rows // 2, 128), jnp.float32),
+            pltpu.VMEM((rows // 2, 128), jnp.bfloat16),
+            pltpu.VMEM((peers * rows // 2, 128), jnp.bfloat16),
             pltpu.VMEM((peers * rows, replicas * rank), jnp.bfloat16),
             pltpu.VMEM((peers * rows, width // peers), jnp.bfloat16),
             dma((6,)),
             dma((peers,)), dma((peers,)), dma((peers,)), dma((peers,)),
+            dma((peers,)), dma((peers,)), dma((peers,)), dma((peers,)), dma((peers,)), dma((peers,)),
             dma((PLANE,)), dma((replicas,)), dma((PLANE,)), dma((replicas,)),
             dma((replicas,)), dma((replicas,)), dma((replicas,)), dma((replicas,)),
             dma((peers,)), dma((peers,)), dma((peers,)), dma((peers,)),

time: 92.5 us -> 103 us (1.11)
  Pallas kernels: 82.6 us -> 93.5 us
    pallas_call x1, Pallas kernels: 70.6 us -> 81.4 us  [gathered_rows(): pl.pallas_call(functools.partial(gathered_kernel, layers), in_specs=[far,...]
where the time goes in v3:
time: 103 us
  Pallas kernels  93.5 us (91%)
  local copies, waits for them, and re-layouts  5.89 us (6%)
  other arithmetic  1.72 us (2%)
    pallas_call x1, Pallas kernels, gathered_rows(): pl.pallas_call(functools.partial(gathered_kernel, layers), in_specs=[far,...  81.4 us
    pallas_call x1, Pallas kernels, attend(): pl.pallas_call(attend_kernel, grid=(steps,), in_specs=[small, small, wide...  12 us
    unnamed x14, local copies, waits for them, and re-layouts  3.69 us
  transfers between devices with their start and end apart: 1, of which 1 were waited for; matrix products, arithmetic and copies ran while one was open for 1% of the time, Pallas kernels for 0%

profile of v3, /device:TPU:0, one launch (start us, length us, event | category | flops | bytes accessed | tf_op | source)
XLA Modules:
  0.0 102.9 jit_solution(6917432201663231468)
XLA Ops:
  0.0 0.7 broadcast_in_dim.34
  0.7 0.7 broadcast_in_dim.36
  1.5 0.8 select_reduce_fusion
  2.2 0.0 copy-start.3
  2.3 1.4 %copy-done.3 = bf16[96,8192]{1,0:T(8,128)(2,1)S(1)} copy-done((bf16[96,8192]{1,0:T(8,128)(2,1)S(1)}, bf16[96,8192]{1,0:T(8,128)(2,1)}, u32[]{:S(2)}) %copy-start.3) | copy-done | bytes 1572888
  3.7 0.0 copy-start.4
  3.7 1.2 %copy-done.4 = bf16[1,8192,64]{1,2,0:T(8,128)(2,1)S(1)} copy-done((bf16[1,8192,64]{1,2,0:T(8,128)(2,1)S(1)}, bf16[1,8192,64]{1,2,0:T(8,128)(2,1)}, u32[]{:S(2)}) %copy-start.4) | copy-done | bytes 1048600
  4.9 0.0 copy-start.5
  4.9 1.0 %copy-done.5 = bf16[1,64,4096]{2,1,0:T(8,128)(2,1)S(1)} copy-done((bf16[1,64,4096]{2,1,0:T(8,128)(2,1)S(1)}, bf16[1,64,4096]{2,1,0:T(8,128)(2,1)}, u32[]{:S(2)}) %copy-start.5) | copy-done | bytes 524312
  5.9 0.0 copy-start
  5.9 0.0 copy-start.1
  5.9 0.0 copy-start.2
  5.9 81.4 %shard_map.109.d_ref = bf16[96,4096]{1,0:T(8,128)(2,1)S(1)} custom-call(bf16[96,8192]{1,0:T(8,128)(2,1)S(1)} %copy-done.3, s32[8,128]{1,0:T(8,128)S(1)} %broadcast_in_dim.40.st_ref, bf16[64,8192]{1,0:T(8,128)(2,1)S(1)} %bitcast.10, bf16[64,4096]{1,0:T(8,128)(2,1)S(1)} %bitcast.11), custom_call_target="tpu_custom_call" | custom-call | flops 2415919104 | bytes 3932160 | tf_op jit(solution)/shard_map/pallas_call | solution.py:576
  87.4 0.1 broadcast_in_dim.35.lengths_ref
  87.4 0.1 broadcast_in_dim.37.joins_ref
  87.5 0.0 copy-done
  87.5 0.0 copy-done.1
  87.5 0.0 copy-done.2
  87.5 0.0 copy-start.6
  87.6 12.0 %shard_map.110 = bf16[96,4096]{1,0:T(8,128)(2,1)S(1)} custom-call(s32[6,16,128]{2,1,0:T(8,128)S(1)} %broadcast_in_dim.35.lengths_ref, s32[6,16,128]{2,1,0:T(8,128)S(1)} %broadcast_in_dim.37.joins_ref, bf16[96,4096]{1,0:T(8,128)(2,1)S(1)} %copy-done.2, bf16[96,4096]{1,0:T(8,128)(2,1)S(1)} %shard_map.109.d_ref, bf16[3072,512]{1,0:T(8,128)(2,1)S(1)} %bitcast.8, ...), custom_call_target="tpu_custom_call" | custom-call | flops 603979776 | bytes 8650752 | tf_op jit(solution)/shard_map/pallas_call | solution.py:83
  99.6 0.4 collective-permute-start
  100.0 0.0 copy-done.6
  100.0 0.6 dynamic_slice.4
  101.3 0.7 collective-permute-done
  102.0 1.0 broadcast_select_fusion
  (2 shorter events, 0.0 us)
Async XLA Ops:
  2.2 1.4 %copy-start.3 = (bf16[96,8192]{1,0:T(8,128)(2,1)S(1)}, bf16[96,8192]{1,0:T(8,128)(2,1)}, u32[]{:S(2)}) copy-start(bf16[96,8192]{1,0:T(8,128)(2,1)} %h_ref.1) | copy-start | bytes 4718596
  3.7 1.2 %copy-start.4 = (bf16[1,8192,64]{1,2,0:T(8,128)(2,1)S(1)}, bf16[1,8192,64]{1,2,0:T(8,128)(2,1)}, u32[]{:S(2)}) copy-start(bf16[1,8192,64]{1,2,0:T(8,128)(2,1)} %param.20) | copy-start | bytes 3145732
  4.9 1.0 %copy-start.5 = (bf16[1,64,4096]{2,1,0:T(8,128)(2,1)S(1)}, bf16[1,64,4096]{2,1,0:T(8,128)(2,1)}, u32[]{:S(2)}) copy-start(bf16[1,64,4096]{2,1,0:T(8,128)(2,1)} %param.21) | copy-start | bytes 1572868
  5.9 81.6 %copy-start = (bf16[96,32,512]{2,1,0:T(8,128)(2,1)S(1)}, bf16[96,32,512]{2,1,0:T(8,128)(2,1)}, u32[]{:S(2)}) copy-start(bf16[96,32,512]{2,1,0:T(8,128)(2,1)} %param.13) | copy-start | bytes 9437188
  5.9 81.6 %copy-start.1 = (bf16[96,32,512]{2,1,0:T(8,128)(2,1)S(1)}, bf16[96,32,512]{2,1,0:T(8,128)(2,1)}, u32[]{:S(2)}) copy-start(bf16[96,32,512]{2,1,0:T(8,128)(2,1)} %param.14) | copy-start | bytes 9437188
  5.9 81.6 %copy-start.2 = (bf16[96,4096]{1,0:T(8,128)(2,1)S(1)}, bf16[96,4096]{1,0:T(8,128)(2,1)}, u32[]{:S(2)}) copy-start(bf16[96,4096]{1,0:T(8,128)(2,1)} %q_ref.1) | copy-start | bytes 2359300
  87.5 12.5 %copy-start.6 = (s32[8]{0:T(128)S(1)}, s32[8]{0:T(128)}, u32[]{:S(2)}) copy-start(s32[8]{0:T(128)} %param.19) | copy-start | bytes 100
  99.6 2.4 %collective-permute-start = (bf16[96,4096]{1,0:T(8,128)(2,1)S(1)}, bf16[96,4096]{1,0:T(8,128)(2,1)S(1)}, u32[]{:S(2)}, u32[]{:S(2)}) collective-permute-start(bf16[96,4096]{1,0:T(8,128)(2,1)S(1)} %shard_map.110), channel_id=1, source_target_pairs={{0,1},{1,0},{2,3},{3,2},{4,5},{5,4},{6,7},{7,6},{8,9},{9,8},{10,11... | collective-permute-start | bytes 2359304 | tf_op jit(solution)/shard_map/ppermute | solution.py:105

commit v4 on v2

--- a/solution.py
+++ b/solution.py
@@ -30,37 +30,41 @@
     column = lax.broadcasted_iota(jnp.int32, (rows, keys), 1)
     own = row_request == column // positions
     position = column % positions
-    halves = []
+    units = [(half, group) for half in range(2) for group in range(KEY_HEADS)]
+    seen = []
     for half in range(2):
         limits = lengths_ref[0, half * HALF_ROWS : (half + 1) * HALF_ROWS, 0:1]
         joins = joins_ref[0, half * HALF_ROWS : (half + 1) * HALF_ROWS, 0:1]
         low = jnp.where(joins == 0, 0, limits - SPAN)
         limits = jnp.concatenate([limits] * per_group, axis=0)
         low = jnp.concatenate([low] * per_group, axis=0)
-        visible = own & (position < limits) & (position >= low)
-        outs = []
-        for group in range(KEY_HEADS):
-            lanes = pl.ds(group * HEAD_WIDTH, HEAD_WIDTH)
-            key_block = k_ref[pl.ds(half * keys, keys), lanes]
-            value_block = v_ref[pl.ds(half * keys, keys), lanes]
-            pieces = []
-            for ref in (q_ref, d_ref):
-                for head in range(per_group):
-                    at = (group * per_group + head) * HEAD_WIDTH
-                    piece = ref[:, pl.ds(at, HEAD_WIDTH)].astype(jnp.float32)
-                    pieces.append(piece[half * HALF_ROWS : (half + 1) * HALF_ROWS])
-            queries = jnp.concatenate(pieces, axis=0).astype(jnp.bfloat16)
-            both = lax.dot_general(
-                queries, key_block, (((1,), (1,)), ((), ())), preferred_element_type=jnp.float32
-            )
-            scores = (both[:rows] + both[rows:]) * scale
-            scores = jnp.where(visible, scores, NEG_LARGE)
-            top = jnp.max(scores, axis=1, keepdims=True)
-            raised = jnp.where(visible, jnp.exp(scores - top), 0.0)
-            total = jnp.sum(raised, axis=1, keepdims=True)
-            weights = (raised / total).astype(jnp.bfloat16)
-            outs.append(jnp.dot(weights, value_block, preferred_element_type=jnp.float32))
-        halves.append(outs)
+        seen.append(own & (position < limits) & (position >= low))
+    scored = []
+    for half, group in units:
+        key_block = k_ref[pl.ds(half * keys, keys), pl.ds(group * HEAD_WIDTH, HEAD_WIDTH)]
+        pieces = []
+        for ref in (q_ref, d_ref):
+            for head in range(per_group):
+                at = (group * per_group + head) * HEAD_WIDTH
+                piece = ref[:, pl.ds(at, HEAD_WIDTH)].astype(jnp.float32)
+                pieces.append(piece[half * HALF_ROWS : (half + 1) * HALF_ROWS])
+        queries = jnp.concatenate(pieces, axis=0).astype(jnp.bfloat16)
+        both = lax.dot_general(
+            queries, key_block, (((1,), (1,)), ((), ())), preferred_element_type=jnp.float32
+        )
+        scores = (both[:rows] + both[rows:]) * scale
+        scored.append(jnp.where(seen[half], scores, NEG_LARGE))
+    tops = [jnp.max(scores, axis=1, keepdims=True) for scores in scored]
+    raised = [
+        jnp.where(seen[half], jnp.exp(scores - top), 0.0)
+        for (half, _), scores, top in zip(units, scored, tops)
+    ]
+    totals = [jnp.sum(lifted, axis=1, keepdims=True) for lifted in raised]
+    halves = [[], []]
+    for (half, group), lifted, total in zip(units, raised, totals):
+        value_block = v_ref[pl.ds(half * keys, keys), pl.ds(group * HEAD_WIDTH, HEAD_WIDTH)]
+        weights = (lifted / total).astype(jnp.bfloat16)
+        halves[half].append(jnp.dot(weights, value_block, preferred_element_type=jnp.float32))
     for group in range(KEY_HEADS):
         for head in range(per_group):
             at = (group * per_group + head) * HEAD_WIDTH
@@ -118,7 +122,7 @@
 
 def gathered_kernel(
     layers, h_ref, st_ref, down_ref, up_ref, out_ref,
-    h_buf, st_buf, down_buf, up_buf, part, part_in, narrow, narrow_all, spread, wide,
+    h_buf, st_buf, tags, down_buf, up_buf, part, packed, part_in, narrow, narrow_all, spread, wide,
     local_sem, h_send, h_recv, st_send, st_recv,
     down_send, down_recv, up_send, up_recv, climb_send, sink_send, climb_up_send, sink_up_send,
     part_send, part_recv, narrow_send, narrow_recv, wide_send, wide_recv,
@@ -131,6 +135,7 @@
     side, core = local // 2, local % 2
     me = group * PLANE + local
     peers = 2 * PLANE
+    packs = rows // 2
 
     def peer(i):
         g = (group + i // 4) % 2
@@ -180,6 +185,9 @@
     def stored(buf, a):
         return buf.at[pl.ds(a * rank, rank), :]
 
+    def tag_rows(ref, j):
+        return ref.at[pl.ds(j * 8, 8), :]
+
     def piece(ref, j, size):
         return ref.at[:, pl.ds(j * size, size)]
 
@@ -190,7 +198,7 @@
         pltpu.make_async_copy(piece(down_ref, me, depth), stored(down_buf, here), local_sem.at[0]),
         pltpu.make_async_copy(piece(up_ref, me, lanes), stored(up_buf, here), local_sem.at[1]),
         pltpu.make_async_copy(piece(h_ref, me, depth), block(h_buf, me), local_sem.at[2]),
-        pltpu.make_async_copy(st_ref, block(st_buf, me), local_sem.at[3]),
+        pltpu.make_async_copy(st_ref, tag_rows(st_buf, me), local_sem.at[3]),
     ]
     for copy in mine:
         copy.start()
@@ -217,60 +225,70 @@
 
     def st_copy(g, l, j):
         return push(
-            st_ref, block(st_buf, me), st_send.at[j], st_recv.at[me], g, layer * PLANE + l
+            st_ref, tag_rows(st_buf, me), st_send.at[j], st_recv.at[me], g, layer * PLANE + l
         )
 
     over_locals(lambda l: down_copy(l).start(), 1)
     mine[0].wait()
     mine[1].wait()
 
-    def onward(buf, a, send, recv, step):
-        return push(
-            stored(buf, a), stored(buf, a), send.at[a], recv.at[a], group, here + step * PLANE
-        )
-
-    def arrived(buf, a, recv):
-        push(stored(buf, a), stored(buf, a), local_sem.at[4], recv.at[a], group, here).wait_recv()
+    def onward(buf, a, send, recv, step, view):
+        return push(
+            view(buf, a), view(buf, a), send.at[a], recv.at[a], group, here + step * PLANE
+        )
+
+    def arrived(buf, a, recv, view):
+        push(view(buf, a), view(buf, a), local_sem.at[4], recv.at[a], group, here).wait_recv()
+
+    def hop(buf, a, send, recv, step, do):
+        do(onward(buf, a, send, recv, step, stored))
+
+    def start(copy):
+        copy.start()
 
     def first_hop(buf, recv, climb, sink, l):
         a = layer * PLANE + l
 
         @pl.when(l != local)
         def _():
-            arrived(buf, a, recv)
+            arrived(buf, a, recv, stored)
 
         @pl.when(layer < layers - 1)
         def _():
-            onward(buf, a, climb, recv, 1).start()
+            hop(buf, a, climb, recv, 1, start)
 
         @pl.when(layer > 0)
         def _():
-            onward(buf, a, sink, recv, -1).start()
+            hop(buf, a, sink, recv, -1, start)
+
+    def landed(buf, a, recv):
+        arrived(buf, a, recv, stored)
 
     def later_hop(buf, recv, climb, sink, t, l):
         @pl.when(layer - t >= 0)
         def _():
             a = (layer - t) * PLANE + l
-            arrived(buf, a, recv)
+            landed(buf, a, recv)
 
             @pl.when(layer < layers - 1)
             def _():
-                onward(buf, a, climb, recv, 1).start()
+                hop(buf, a, climb, recv, 1, start)
 
         @pl.when(layer + t < layers)
         def _():
             a = (layer + t) * PLANE + l
-            arrived(buf, a, recv)
+            landed(buf, a, recv)
 
             @pl.when(layer > 0)
             def _():
-                onward(buf, a, sink, recv, -1).start()
+                hop(buf, a, sink, recv, -1, start)
 
     downs = (down_buf, down_recv, climb_send, sink_send)
     ups = (up_buf, up_recv, climb_up_send, sink_up_send)
     first_hop(*downs, local)
     over_peers(lambda g, l, j: st_copy(g, l, j).start())
     over_locals(lambda l: first_hop(*downs, l), 1)
+
     over_peers(lambda g, l, j: h_copy(g, l, j).start())
     over_locals(lambda l: up_copy(l).start(), 1)
     for t in range(1, layers - 1):
@@ -282,59 +300,86 @@
     def here_recv(src, dst, recv, g, l):
         push(src, dst, local_sem.at[4], recv, g, layer * PLANE + l).wait_recv()
 
-    over_peers(lambda g, l, j: here_recv(block(h_buf, j), block(h_buf, j), h_recv.at[j], g, l))
-    over_peers(lambda g, l, j: here_recv(block(st_buf, j), block(st_buf, j), st_recv.at[j], g, l))
+    def taken(view, recv):
+        return lambda g, l, j: here_recv(view(j), view(j), recv.at[j], g, l)
+
+    def tagged(src, dst):
+        for j in range(peers):
+            row = src[j * 8 : j * 8 + 1, :].astype(jnp.float32)
+            turned = jnp.transpose(jnp.broadcast_to(row, (128, 128)))
+            dst[j * rows : (j + 1) * rows, :] = turned[:rows].astype(jnp.int32)
+
+    over_peers(taken(lambda j: tag_rows(st_buf, j), st_recv))
+    tagged(st_buf, tags)
+
+    over_peers(taken(lambda j: block(h_buf, j), h_recv))
     over_locals(lambda l: later_hop(*downs, layers - 1, l))
 
     lane = lax.broadcasted_iota(jnp.int32, (1, 2 * rank), 1) // rank
-    part[...] = jnp.zeros_like(part)
-
-    def narrowed(s, carry):
-        at = pl.ds(s * 4 * rank, 4 * rank)
-        both = lax.dot_general(
-            h_buf[...], down_buf[at, :], (((1,), (1,)), ((), ())),
-            preferred_element_type=jnp.float32,
-        )
-        stores = st_buf[...]
-        kept = jnp.where(stores == s * 4 + lane, both[:, : 2 * rank], 0.0)
-        kept = kept + jnp.where(stores == s * 4 + 2 + lane, both[:, 2 * rank :], 0.0)
-        part[...] += kept
-        return carry
-
-    lax.fori_loop(0, down_buf.shape[0] // (4 * rank), narrowed, 0)
+
+    def products(left, right, stores_ref, to):
+        part[...] = jnp.zeros_like(part)
+
+        def narrowed(s, carry):
+            at = pl.ds(s * 4 * rank, 4 * rank)
+            both = lax.dot_general(
+                left[...], right[at, :], (((1,), (1,)), ((), ())),
+                preferred_element_type=jnp.float32,
+            )
+            stores = stores_ref[...]
+            kept = jnp.where(stores == s * 4 + lane, both[:, : 2 * rank], 0.0)
+            kept = kept + jnp.where(stores == s * 4 + 2 + lane, both[:, 2 * rank :], 0.0)
+            part[...] += kept
+            return carry
+
+        lax.fori_loop(0, down_buf.shape[0] // (4 * rank), narrowed, 0)
+        summed = part[...]
+        summed = summed + pltpu.roll(summed, rank, 1)
+        for j in range(peers):
+            first = summed[j * rows : j * rows + packs]
+            second = summed[j * rows + packs : (j + 1) * rows]
+            to[j * packs : (j + 1) * packs, :] = jnp.where(lane == 0, first, second)
+
+    def packs_of(ref, j):
+        return ref.at[pl.ds(j * packs, packs), :]
 
     def part_copy(g, l, j):
         return push(
-            block(part, j), part_in.at[me], part_send.at[j], part_recv.at[me],
+            packs_of(packed, j), part_in.at[me], part_send.at[j], part_recv.at[me],
             g, layer * PLANE + l,
         )
 
+    products(h_buf, down_buf, tags, packed)
     over_peers(lambda g, l, j: part_copy(g, l, j).start())
     for t in range(1, layers - 1):
         over_locals(lambda l: later_hop(*ups, t, l))
-    over_peers(lambda g, l, j: here_recv(part_in.at[j], part_in.at[j], part_recv.at[j], g, l))
-    part_in[me] = part[pl.ds(me * rows, rows), :]
+    over_peers(taken(lambda j: part_in.at[j], part_recv))
+    part_in[me] = packed[pl.ds(me * packs, packs), :]
     total = part_in[0]
     for j in range(1, peers):
         total = total + part_in[j]
-    total = total + pltpu.roll(total, rank, 1)
     narrow[...] = total.astype(jnp.bfloat16)
 
     def narrow_copy(g, l, j):
         return push(
-            narrow, block(narrow_all, me), narrow_send.at[j], narrow_recv.at[me],
+            narrow, packs_of(narrow_all, me), narrow_send.at[j], narrow_recv.at[me],
             g, layer * PLANE + l,
         )
 
     over_peers(lambda g, l, j: narrow_copy(g, l, j).start())
-    narrow_all[pl.ds(me * rows, rows), :] = narrow[...]
-    over_peers(
-        lambda g, l, j: here_recv(block(narrow_all, j), block(narrow_all, j), narrow_recv.at[j], g, l)
-    )
-    for s in range(spread.shape[1] // (2 * rank)):
-        spread[:, s * 2 * rank : (s + 1) * 2 * rank] = jnp.where(
-            st_buf[...] == 2 * s + lane, narrow_all[...].astype(jnp.float32), 0.0
-        ).astype(jnp.bfloat16)
+    narrow_all[pl.ds(me * packs, packs), :] = narrow[...]
+    over_peers(taken(lambda j: packs_of(narrow_all, j), narrow_recv))
+    for j in range(peers):
+        pair = narrow_all[j * packs : (j + 1) * packs, :].astype(jnp.float32)
+        turned = pltpu.roll(pair, rank, 1)
+        own = jnp.concatenate(
+            [jnp.where(lane == 0, pair, turned), jnp.where(lane == 0, turned, pair)], axis=0
+        )
+        stores = tags[j * rows : (j + 1) * rows, :]
+        for s in range(spread.shape[1] // (2 * rank)):
+            spread[j * rows : (j + 1) * rows, s * 2 * rank : (s + 1) * 2 * rank] = jnp.where(
+                stores == 2 * s + lane, own, 0.0
+            ).astype(jnp.bfloat16)
     over_locals(lambda l: later_hop(*ups, layers - 1, l))
 
     def widened(c, carry):
@@ -376,19 +421,22 @@
 
     over_peers(left_peer)
 
+    def sent(copy):
+        copy.wait_send()
+
     def passed(s, carry):
         def one(l):
             a = s * PLANE + l
 
             @pl.when((layer < layers - 1) & (s <= layer))
             def _():
-                onward(down_buf, a, climb_send, down_recv, 1).wait_send()
-                onward(up_buf, a, climb_up_send, up_recv, 1).wait_send()
+                hop(down_buf, a, climb_send, down_recv, 1, sent)
+                hop(up_buf, a, climb_up_send, up_recv, 1, sent)
 
             @pl.when((layer > 0) & (s >= layer))
             def _():
-                onward(down_buf, a, sink_send, down_recv, -1).wait_send()
-                onward(up_buf, a, sink_up_send, up_recv, -1).wait_send()
+                hop(down_buf, a, sink_send, down_recv, -1, sent)
+                hop(up_buf, a, sink_up_send, up_recv, -1, sent)
 
         over_locals(one)
         return carry
@@ -403,9 +451,10 @@
     layers = replicas // PLANE
     peers = 2 * PLANE
     down = jnp.swapaxes(down_factors[0], 0, 1)
-    tags = jnp.broadcast_to(stores[:, None], (rows, 128))
+    tags = jnp.broadcast_to(jnp.pad(stores, (0, 128 - rows))[None, :], (8, 128))
     dma = pltpu.SemaphoreType.DMA
     here = pl.BlockSpec(memory_space=pltpu.VMEM)
+    far = pl.BlockSpec(memory_space=pl.ANY)
     return pl.pallas_call(
         functools.partial(gathered_kernel, layers),
         in_specs=[here] * 4,
@@ -413,13 +462,15 @@
         out_shape=jax.ShapeDtypeStruct((rows, width), jnp.bfloat16),
         scratch_shapes=[
             pltpu.VMEM((peers * rows, depth // peers), jnp.bfloat16),
+            pltpu.VMEM((peers * 8, 128), jnp.int32),
             pltpu.VMEM((peers * rows, 128), jnp.int32),
             pltpu.VMEM((replicas * rank, depth // peers), jnp.bfloat16),
             pltpu.VMEM((replicas * rank, width // peers), jnp.bfloat16),
             pltpu.VMEM((peers * rows, 128), jnp.float32),
-            pltpu.VMEM((peers, rows, 128), jnp.float32),
-            pltpu.VMEM((rows, 128), jnp.bfloat16),
-            pltpu.VMEM((peers * rows, 128), jnp.bfloat16),
+            pltpu.VMEM((peers * rows // 2, 128), jnp.float32),
+            pltpu.VMEM((peers, rows // 2, 128), jnp.float32),
+            pltpu.VMEM((rows // 2, 128), jnp.bfloat16),
+            pltpu.VMEM((peers * rows // 2, 128), jnp.bfloat16),
             pltpu.VMEM((peers * rows, replicas * rank), jnp.bfloat16),
             pltpu.VMEM((peers * rows, width // peers), jnp.bfloat16),
             dma((6,)),

time: 92.5 us -> 83.8 us (0.906)
  Pallas kernels: 82.6 us -> 73.7 us
    pallas_call x1, Pallas kernels: 12 us -> 3.88 us  [attend(): pl.pallas_call(attend_kernel, grid=(steps,), in_specs=[small, small, wide...]
where the time goes in v4:
time: 83.8 us; the launch traced here: 83.6 us
  Pallas kernels  73.7 us (88%)
  local copies, waits for them, and re-layouts  5.89 us (7%)
  other arithmetic  1.72 us (2%)
  starting transfers between devices  0.9 us (1%)
    pallas_call x1, Pallas kernels, gathered_rows(): pl.pallas_call(functools.partial(gathered_kernel, layers), in_specs=[here...  69.8 us
    pallas_call x1, Pallas kernels, attend(): pl.pallas_call(attend_kernel, grid=(steps,), in_specs=[small, small, wide...  3.88 us
    unnamed x14, local copies, waits for them, and re-layouts  3.69 us
  transfers between devices with their start and end apart: 1, of which 1 were waited for; matrix products, arithmetic and copies ran while one was open for 1% of the time, Pallas kernels for 0%

profile of v4, /device:TPU:0, one launch (start us, length us, event | category | flops | bytes accessed | tf_op | source)
XLA Modules:
  0.0 83.6 jit_solution(15134358463244157105)
XLA Ops:
  0.0 0.7 broadcast_in_dim.34
  0.7 0.7 broadcast_in_dim.36
  1.5 0.8 select_reduce_fusion
  2.2 0.0 copy-start.3
  2.3 1.4 %copy-done.3 = bf16[96,8192]{1,0:T(8,128)(2,1)S(1)} copy-done((bf16[96,8192]{1,0:T(8,128)(2,1)S(1)}, bf16[96,8192]{1,0:T(8,128)(2,1)}, u32[]{:S(2)}) %copy-start.3) | copy-done | bytes 1572888
  3.7 0.0 copy-start.4
  3.7 1.2 %copy-done.4 = bf16[1,8192,64]{1,2,0:T(8,128)(2,1)S(1)} copy-done((bf16[1,8192,64]{1,2,0:T(8,128)(2,1)S(1)}, bf16[1,8192,64]{1,2,0:T(8,128)(2,1)}, u32[]{:S(2)}) %copy-start.4) | copy-done | bytes 1048600
  4.9 0.0 copy-start.5
  4.9 1.0 %copy-done.5 = bf16[1,64,4096]{2,1,0:T(8,128)(2,1)S(1)} copy-done((bf16[1,64,4096]{2,1,0:T(8,128)(2,1)S(1)}, bf16[1,64,4096]{2,1,0:T(8,128)(2,1)}, u32[]{:S(2)}) %copy-start.5) | copy-done | bytes 524312
  5.9 0.0 copy-start
  5.9 0.0 copy-start.1
  5.9 0.0 copy-start.2
  5.9 69.8 %shard_map.109.d_ref = bf16[96,4096]{1,0:T(8,128)(2,1)S(1)} custom-call(bf16[96,8192]{1,0:T(8,128)(2,1)S(1)} %copy-done.3, s32[8,128]{1,0:T(8,128)S(1)} %broadcast_in_dim.40.st_ref, bf16[64,8192]{1,0:T(8,128)(2,1)S(1)} %bitcast.10, bf16[64,4096]{1,0:T(8,128)(2,1)S(1)} %bitcast.11), custom_call_target="tpu_custom_call" | custom-call | flops 2415919104 | bytes 3932160 | tf_op jit(solution)/shard_map/pallas_call | solution.py:458
  75.7 0.1 broadcast_in_dim.35.lengths_ref
  75.8 0.1 broadcast_in_dim.37.joins_ref
  75.9 0.0 copy-done
  75.9 0.0 copy-done.1
  75.9 0.0 copy-done.2
  75.9 0.0 copy-start.6
  75.9 3.9 %shard_map.110 = bf16[96,4096]{1,0:T(8,128)(2,1)S(1)} custom-call(s32[6,16,128]{2,1,0:T(8,128)S(1)} %broadcast_in_dim.35.lengths_ref, s32[6,16,128]{2,1,0:T(8,128)S(1)} %broadcast_in_dim.37.joins_ref, bf16[96,4096]{1,0:T(8,128)(2,1)S(1)} %copy-done.2, bf16[96,4096]{1,0:T(8,128)(2,1)S(1)} %shard_map.109.d_ref, bf16[3072,512]{1,0:T(8,128)(2,1)S(1)} %bitcast.8, ...), custom_call_target="tpu_custom_call" | custom-call | flops 603979776 | bytes 8650752 | tf_op jit(solution)/shard_map/pallas_call | solution.py:87
  79.8 0.9 %collective-permute-start = (bf16[96,4096]{1,0:T(8,128)(2,1)S(1)}, bf16[96,4096]{1,0:T(8,128)(2,1)S(1)}, u32[]{:S(2)}, u32[]{:S(2)}) collective-permute-start(bf16[96,4096]{1,0:T(8,128)(2,1)S(1)} %shard_map.110), channel_id=1, source_target_pairs={{0,1},{1,0},{2,3},{3,2},{4,5},{5,4},{6,7},{7,6},{8,9},{9,8},{10,11... | collective-permute-start | bytes 2359304 | tf_op jit(solution)/shard_map/ppermute | solution.py:109
  80.7 0.0 copy-done.6
  80.7 0.6 dynamic_slice.4
  81.9 0.7 collective-permute-done
  82.6 1.0 %broadcast_select_fusion = bf16[96,4096]{1,0:T(8,128)(2,1)} fusion(bf16[96,4096]{1,0:T(8,128)(2,1)S(1)} %collective-permute-done, bf16[96,4096]{1,0:T(8,128)(2,1)S(1)} %shard_map.110, pred[]{:T(512)} %bitcast), kind=kLoop, calls=%fused_computation | loop fusion | flops 393216 | bytes 2359297 | tf_op jit(solution)/shard_map/jit(_where)/select_n | solution.py:552
  (2 shorter events, 0.0 us)
Async XLA Ops:
  2.2 1.4 %copy-start.3 = (bf16[96,8192]{1,0:T(8,128)(2,1)S(1)}, bf16[96,8192]{1,0:T(8,128)(2,1)}, u32[]{:S(2)}) copy-start(bf16[96,8192]{1,0:T(8,128)(2,1)} %h_ref.1) | copy-start | bytes 4718596
  3.7 1.2 %copy-start.4 = (bf16[1,8192,64]{1,2,0:T(8,128)(2,1)S(1)}, bf16[1,8192,64]{1,2,0:T(8,128)(2,1)}, u32[]{:S(2)}) copy-start(bf16[1,8192,64]{1,2,0:T(8,128)(2,1)} %param.20) | copy-start | bytes 3145732
  4.9 1.0 %copy-start.5 = (bf16[1,64,4096]{2,1,0:T(8,128)(2,1)S(1)}, bf16[1,64,4096]{2,1,0:T(8,128)(2,1)}, u32[]{:S(2)}) copy-start(bf16[1,64,4096]{2,1,0:T(8,128)(2,1)} %param.21) | copy-start | bytes 1572868
  5.9 70.0 %copy-start = (bf16[96,32,512]{2,1,0:T(8,128)(2,1)S(1)}, bf16[96,32,512]{2,1,0:T(8,128)(2,1)}, u32[]{:S(2)}) copy-start(bf16[96,32,512]{2,1,0:T(8,128)(2,1)} %param.13) | copy-start | bytes 9437188
  5.9 70.0 %copy-start.1 = (bf16[96,32,512]{2,1,0:T(8,128)(2,1)S(1)}, bf16[96,32,512]{2,1,0:T(8,128)(2,1)}, u32[]{:S(2)}) copy-start(bf16[96,32,512]{2,1,0:T(8,128)(2,1)} %param.14) | copy-start | bytes 9437188
  5.9 70.0 %copy-start.2 = (bf16[96,4096]{1,0:T(8,128)(2,1)S(1)}, bf16[96,4096]{1,0:T(8,128)(2,1)}, u32[]{:S(2)}) copy-start(bf16[96,4096]{1,0:T(8,128)(2,1)} %q_ref.1) | copy-start | bytes 2359300
  75.9 4.8 %copy-start.6 = (s32[8]{0:T(128)S(1)}, s32[8]{0:T(128)}, u32[]{:S(2)}) copy-start(s32[8]{0:T(128)} %param.19) | copy-start | bytes 100
  79.8 2.8 %collective-permute-start = (bf16[96,4096]{1,0:T(8,128)(2,1)S(1)}, bf16[96,4096]{1,0:T(8,128)(2,1)S(1)}, u32[]{:S(2)}, u32[]{:S(2)}) collective-permute-start(bf16[96,4096]{1,0:T(8,128)(2,1)S(1)} %shard_map.110), channel_id=1, source_target_pairs={{0,1},{1,0},{2,3},{3,2},{4,5},{5,4},{6,7},{7,6},{8,9},{9,8},{10,11... | collective-permute-start | bytes 2359304 | tf_op jit(solution)/shard_map/ppermute | solution.py:109
